TPU v7x, 32 devices: a whole 2x2x4 slice. The times are simulated.
32 devices in a mesh: head: 2 (over y), inner: 4 (over x, core), outer: 4 (over z).
Axes of the slice: x: 2, y: 2, z: 4, core: 2. Of those that a mesh axis runs over, the one named last changes fastest.
Arguments:
- query: bfloat16 [4, 4, 256, 4096], P('outer', 'inner', 'head'), may hold values from -300 to 300
- dout: bfloat16 [4, 4, 256, 4096], P('outer', 'inner', 'head'), may hold values from -6 to 6
- key_mant: bfloat16 [4, 4, 256, 512], P('outer', 'inner', None, 'head'), may hold values from -6 to 6
- value_mantissas: bfloat16 [4, 4, 256, 512], P('outer', 'inner', None, 'head'), may hold values from -6 to 6
- key_exps: int32 [4, 4, 2, 4], P('outer', 'inner', None, 'head'), may hold values from -1 to 1
- value_exponents: int32 [4, 4, 2, 4], P('outer', 'inner', None, 'head'), may hold values from -1 to 1
- reach: int32 [4, 4], P('outer', 'inner'), may hold values from 64 to 256
Outputs:
- query_grad: bfloat16 [4, 4, 256, 4096], P('outer', 'inner', 'head')
- key_grad: bfloat16 [4, 4, 256, 512], P('outer', 'inner', None, 'head')
- value_grad: bfloat16 [4, 4, 256, 512], P('outer', 'inner', None, 'head')
All inputs are finite; a program needn't handle non-finite values.
Results may differ from a plain program's by a relative error of at most 0.013.
Values may be sent and summed in bfloat16 or wider, within the bound.
A program may use at most 64 MiB of HBM per device.

v0:
```python
import jax
import jax.numpy as jnp
from jax import lax
from jax.sharding import PartitionSpec as P

QUERY_HEADS = 32
KEY_VALUE_HEADS = 4
HEAD_SIZE = 128


NEG_FILL = -1e30


def passed_along(value, axis, steps):
    count = lax.axis_size(axis)
    initial, last = (max(0, -steps), min(count, count - steps))
    return lax.ppermute(value, axis, [(source, source + steps) for source in range(initial, last)])


def expand(mantissa_values, scale_factors):
    blocks, head_count = scale_factors.shape
    length, row_width = mantissa_values.shape
    reshaped_array = mantissa_values.reshape(
        blocks, length // blocks, head_count, row_width // head_count
    )
    return (reshaped_array * scale_factors[:, None, :, None]).reshape(
        length, head_count, row_width // head_count
    )


def attend(
    queries, grads_out, own_keys, own_values, prev_keys, prev_values, first_cycle, reach_rows
):
    query_matrix = queries.shape[0]
    length = own_keys.shape[0]
    factor = HEAD_SIZE ** (-0.5)
    positions = jnp.arange(query_matrix)
    columns = jnp.arange(length)
    own_mask = columns[None, :] <= positions[:, None]
    prev_mask = jnp.logical_and(columns >= length - reach_rows, jnp.logical_not(first_cycle))

    def per_head(members):
        query_head, grad_head, key_own, value_own, key_prev, value_prev = members
        score_own = (
            jnp.einsum("tgd,sd->gts", query_head, key_own, preferred_element_type=jnp.float32)
            * factor
        )
        score_prev = (
            jnp.einsum("tgd,sd->gts", query_head, key_prev, preferred_element_type=jnp.float32)
            * factor
        )
        score_own = jnp.where(own_mask[None], score_own, NEG_FILL)
        score_prev = jnp.where(prev_mask[None, None], score_prev, NEG_FILL)
        row_peak = jnp.maximum(jnp.max(score_own, axis=2), jnp.max(score_prev, axis=2))
        weight_own = jnp.exp(score_own - row_peak[:, :, None])
        weight_prev = jnp.exp(score_prev - row_peak[:, :, None])
        weight_sum = jnp.sum(weight_own, axis=2) + jnp.sum(weight_prev, axis=2)
        weight_own = weight_own / weight_sum[:, :, None]
        weight_prev = weight_prev / weight_sum[:, :, None]
        rounded_own = weight_own.astype(jnp.bfloat16)
        rounded_prev = weight_prev.astype(jnp.bfloat16)
        output = jnp.einsum(
            "gts,sd->gtd", rounded_own, value_own, preferred_element_type=jnp.float32
        ) + jnp.einsum("gts,sd->gtd", rounded_prev, value_prev, preferred_element_type=jnp.float32)
        row_dot = jnp.einsum("tgd,gtd->gt", grad_head.astype(jnp.float32), output)
        dprob_own = jnp.einsum(
            "tgd,sd->gts", grad_head, value_own, preferred_element_type=jnp.float32
        )
        dprob_prev = jnp.einsum(
            "tgd,sd->gts", grad_head, value_prev, preferred_element_type=jnp.float32
        )
        dscore_own = (weight_own * (dprob_own - row_dot[:, :, None])).astype(jnp.bfloat16)
        dscore_prev = (weight_prev * (dprob_prev - row_dot[:, :, None])).astype(jnp.bfloat16)
        query_grad = (
            jnp.einsum("gts,sd->tgd", dscore_own, key_own, preferred_element_type=jnp.float32)
            + jnp.einsum("gts,sd->tgd", dscore_prev, key_prev, preferred_element_type=jnp.float32)
        ) * factor
        key_grad_own = (
            jnp.einsum("gts,tgd->sd", dscore_own, query_head, preferred_element_type=jnp.float32)
            * factor
        )
        key_grad_prev = (
            jnp.einsum("gts,tgd->sd", dscore_prev, query_head, preferred_element_type=jnp.float32)
            * factor
        )
        value_grad_own = jnp.einsum(
            "gts,tgd->sd", rounded_own, grad_head, preferred_element_type=jnp.float32
        )
        value_grad_prev = jnp.einsum(
            "gts,tgd->sd", rounded_prev, grad_head, preferred_element_type=jnp.float32
        )
        return (query_grad, key_grad_own, value_grad_own, key_grad_prev, value_grad_prev)

    stacked = (
        jnp.moveaxis(queries, 1, 0),
        jnp.moveaxis(grads_out, 1, 0),
        jnp.moveaxis(own_keys, 1, 0),
        jnp.moveaxis(own_values, 1, 0),
        jnp.moveaxis(prev_keys, 1, 0),
        jnp.moveaxis(prev_values, 1, 0),
    )
    results = lax.map(per_head, stacked)
    query_grad = jnp.moveaxis(results[0], 0, 1).reshape(query_matrix, -1)
    others = tuple((jnp.moveaxis(member, 0, 1).reshape(1, 1, length, -1) for member in results[1:]))
    return (query_grad,) + others


def on_device(query, dout, key_mant, value_mantissas, key_exps, value_exponents, reach):
    heads_per_group = QUERY_HEADS // KEY_VALUE_HEADS
    key_scales = jnp.exp2(key_exps.astype(jnp.float32)).astype(jnp.bfloat16)
    value_scales = jnp.exp2(value_exponents.astype(jnp.float32)).astype(jnp.bfloat16)
    previous = passed_along((key_mant, value_mantissas, key_scales, value_scales), "inner", 1)
    first_cycle = lax.axis_index("inner") == 0
    reach_rows = reach[0, 0]
    query_heads, grad_heads = (
        lax.all_to_all(query, "head", split_axis=3, concat_axis=2, tiled=True),
        lax.all_to_all(dout, "head", split_axis=3, concat_axis=2, tiled=True),
    )
    length = query_heads.shape[2]
    head_count = key_mant.shape[3] // HEAD_SIZE
    queries = query_heads.reshape(length, head_count, heads_per_group, HEAD_SIZE)
    grads_out = grad_heads.reshape(length, head_count, heads_per_group, HEAD_SIZE)
    own_keys = expand(key_mant[0, 0], key_scales[0, 0])
    own_values = expand(value_mantissas[0, 0], value_scales[0, 0])
    prev_keys = expand(previous[0][0, 0], previous[2][0, 0])
    prev_values = expand(previous[1][0, 0], previous[3][0, 0])
    query_grad, key_own, value_own, key_next, value_next = attend(
        queries, grads_out, own_keys, own_values, prev_keys, prev_values, first_cycle, reach_rows
    )
    rounded = query_grad.astype(jnp.bfloat16).reshape(1, 1, length, -1)
    query_out = lax.all_to_all(rounded, "head", split_axis=2, concat_axis=3, tiled=True)
    returned = passed_along(
        (key_next.astype(jnp.bfloat16), value_next.astype(jnp.bfloat16)), "inner", -1
    )
    key_grad = (key_own + returned[0].astype(jnp.float32)).astype(jnp.bfloat16)
    value_grad = (value_own + returned[1].astype(jnp.float32)).astype(jnp.bfloat16)
    return (query_out, key_grad, value_grad)


def solution(mesh):
    placed = (
        P("outer", "inner", "head", None),
        P("outer", "inner", "head", None),
        P("outer", "inner", None, "head"),
        P("outer", "inner", None, "head"),
        P("outer", "inner", None, "head"),
        P("outer", "inner", None, "head"),
        P("outer", "inner"),
    )
    return jax.shard_map(
        on_device,
        mesh=mesh,
        in_specs=placed,
        out_specs=(
            P("outer", "inner", "head", None),
            P("outer", "inner", None, "head"),
            P("outer", "inner", None, "head"),
        ),
        check_vma=False,
    )
```

profile of v0, /device:TPU:1, one launch (start us, length us, event | category | flops | bytes accessed | tf_op | source)
XLA Modules:
  0.0 164.5 jit_solution(11538260041380829400)
XLA Ops:
  0.6 0.7 exponential_convert_fusion
  1.3 4.5 %collective-permute-start.3 = (bf16[1,1,2,2]{3,2,1,0:T(2,128)(2,1)S(1)}, bf16[1,1,2,2]{3,2,1,0:T(2,128)(2,1)S(1)}, u32[]{:S(2)}, u32[]{:S(2)}) collective-permute-start(bf16[1,1,2,2]{3,2,1,0:T(2,128)(2,1)S(1)} %exponential_convert_fusion), channel_id=1, source_target_pairs={{0,4},{4,8},{8,12},{1,5},{5,9},{9,13},{2,6},{6,10},{10,14},{3,7},{... | collective-permute-start | bytes 32 | tf_op jit(solution)/shard_map/ppermute | solution.py:17
  5.8 0.7 exponential_convert_fusion.1
  6.5 1.9 %collective-permute-start.1 = (bf16[1,1,2,2]{3,2,1,0:T(2,128)(2,1)S(1)}, bf16[1,1,2,2]{3,2,1,0:T(2,128)(2,1)S(1)}, u32[]{:S(2)}, u32[]{:S(2)}) collective-permute-start(bf16[1,1,2,2]{3,2,1,0:T(2,128)(2,1)S(1)} %exponential_convert_fusion.1), channel_id=1, source_target_pairs={{0,4},{4,8},{8,12},{1,5},{5,9},{9,13},{2,6},{6,10},{10,14},{3,7},{... | collective-permute-start | bytes 32 | tf_op jit(solution)/shard_map/ppermute | solution.py:17
  8.4 1.7 %copy.119 = bf16[1,1,256,256]{2,3,1,0:T(8,128)(2,1)} copy(bf16[1,1,256,256]{3,2,1,0:T(8,128)(2,1)} %param.12) | data formatting | bytes 262144 | tf_op args[3]
  10.1 1.9 %collective-permute-start.2 = (bf16[1,1,256,256]{2,3,1,0:T(8,128)(2,1)}, bf16[1,1,256,256]{2,3,1,0:T(8,128)(2,1)}, u32[]{:S(2)}, u32[]{:S(2)}) collective-permute-start(bf16[1,1,256,256]{2,3,1,0:T(8,128)(2,1)} %copy.119), channel_id=1, source_target_pairs={{0,4},{4,8},{8,12},{1,5},{5,9},{9,13},{2,6},{6,10},{10,14},{3,7},{... | collective-permute-start | bytes 393224 | tf_op jit(solution)/shard_map/ppermute | solution.py:17
  12.0 1.7 %copy.113 = bf16[1,1,256,256]{2,3,1,0:T(8,128)(2,1)} copy(bf16[1,1,256,256]{3,2,1,0:T(8,128)(2,1)} %param.11) | data formatting | bytes 262144 | tf_op args[2]
  13.7 1.9 %collective-permute-start = (bf16[1,1,256,256]{2,3,1,0:T(8,128)(2,1)}, bf16[1,1,256,256]{2,3,1,0:T(8,128)(2,1)}, u32[]{:S(2)}, u32[]{:S(2)}) collective-permute-start(bf16[1,1,256,256]{2,3,1,0:T(8,128)(2,1)} %copy.113), channel_id=1, source_target_pairs={{0,4},{4,8},{8,12},{1,5},{5,9},{9,13},{2,6},{6,10},{10,14},{3,7},{... | collective-permute-start | bytes 393224 | tf_op jit(solution)/shard_map/ppermute | solution.py:17
  15.6 5.0 %copy.115 = bf16[1,1,128,4096]{2,1,0,3:T(2,128)(2,1)S(1)} copy(bf16[1,1,128,4096]{3,2,1,0:T(8,128)(2,1)} %param.9) | data formatting | bytes 2097152 | tf_op args[0]
  21.2 22.4 %reduce.2 = bf16[4096,128]{1,0:T(8,128)(2,1)S(1)} reduce(bf16[4096,1,1,128]{3,2,1,0:T(2,128)(2,1)S(1)} %bitcast.306, bf16[]{:T(256)} %broadcast.60), dimensions={1,2}, to_apply=%bitcast.201.reduce_sub_computation | reduce | bytes 2097154
  43.7 1.2 reshape.109
  44.8 3.6 %all-to-all-start = ((bf16[2,2,131072]{2,1,0:T(2,128)(2,1)}), bf16[2,2,131072]{2,1,0:T(2,128)(2,1)S(1)}, u32[]{:S(2)}, u32[]{:S(2)}) async-start(bf16[2,2,131072]{2,1,0:T(2,128)(2,1)} %reshape.109), calls=%async_computation | async-start | bytes 2097152 | tf_op jit(solution)/shard_map/all_to_all | solution.py:116
  49.5 5.0 %copy.121 = bf16[1,1,128,4096]{2,1,0,3:T(2,128)(2,1)S(1)} copy(bf16[1,1,128,4096]{3,2,1,0:T(8,128)(2,1)} %param.10) | data formatting | bytes 2097152 | tf_op args[1]
  54.6 23.4 %reduce.3 = bf16[4096,128]{1,0:T(8,128)(2,1)} reduce(bf16[4096,1,1,128]{3,2,1,0:T(2,128)(2,1)S(1)} %bitcast.308, bf16[]{:T(256)} %broadcast.60), dimensions={1,2}, to_apply=%bitcast.203.reduce_sub_computation | reduce | bytes 2097154
  78.0 2.2 %reshape.111 = bf16[2,2,131072]{2,1,0:T(2,128)(2,1)} reshape(bf16[4096,128]{1,0:T(8,128)(2,1)} %reduce.3) | data formatting | bytes 2097152
  80.1 1.0 multiply_bitcast_fusion.1
  81.4 4.6 %all-to-all-start.1 = ((bf16[2,2,131072]{2,1,0:T(2,128)(2,1)}), bf16[2,2,131072]{2,1,0:T(2,128)(2,1)}, u32[]{:S(2)}, u32[]{:S(2)}) async-start(bf16[2,2,131072]{2,1,0:T(2,128)(2,1)} %reshape.111), calls=%async_computation.1 | async-start | bytes 2097152 | tf_op jit(solution)/shard_map/all_to_all | solution.py:117
  86.2 1.6 multiply_bitcast_fusion
  87.7 0.9 multiply_bitcast_fusion.2
  88.7 0.9 reshape.110
  90.5 8.0 %all-to-all-done.1 = bf16[2,2,131072]{2,1,0:T(2,128)(2,1)} async-done(((bf16[2,2,131072]{2,1,0:T(2,128)(2,1)}), bf16[2,2,131072]{2,1,0:T(2,128)(2,1)}, u32[]{:S(2)}, u32[]{:S(2)}) %all-to-all-start.1) | async-done | bytes 1048608 | tf_op jit(solution)/shard_map/all_to_all | solution.py:117
  98.5 2.0 %reshape.112 = bf16[4096,1,1,128]{3,2,1,0:T(2,128)(2,1)S(1)} reshape(bf16[2,2,131072]{2,1,0:T(2,128)(2,1)} %all-to-all-done.1) | data formatting | bytes 2097152
  100.5 1.1 copy.159
  101.6 1.5 copy.122
  103.3 21.6 %while.19 = (s32[]{:T(128)}, bf16[2,256,8,128]{1,3,2,0:T(8,128)(2,1)}, f32[2,256,128]{2,1,0:T(8,128)}, f32[2,256,128]{2,1,0:T(8,128)}, bf16[2,256,128]{2,1,0:T(8...) while((s32[]{:T(128)}, ...), condition=%wide.region_5.6_spmd.clone, body=%wide.region_0.5_spmd.clone.sunk | while | flops 1631709696 | bytes 56954876 | solution.py:102
  104.6 0.8 fusion.125
  105.5 0.8 fusion.136
  108.2 1.0 fusion.128
  109.2 0.9 fusion.131
  113.2 1.0 copy-done.1
  115.4 0.8 fusion.125
  116.3 0.8 fusion.136
  119.0 1.0 fusion.128
  120.0 0.9 fusion.131
  123.9 1.0 copy-done.1
  124.9 1.0 copy.134
  126.0 4.2 %collective-permute-start.4 = (bf16[1,1,256,256]{3,2,1,0:T(8,128)(2,1)S(1)}, bf16[1,1,256,256]{3,2,1,0:T(8,128)(2,1)S(1)}, u32[]{:S(2)}, u32[]{:S(2)}) collective-permute-start(bf16[1,1,256,256]{3,2,1,0:T(8,128)(2,1)S(1)} %convert_element_type.96), channel_id=1, source_target_pairs={{4,0},{8,4},{12,8},{5,1},{9,5},{13,9},{6,2},{10,6},{14,10},{7,3},{... | collective-permute-start | bytes 393224 | tf_op jit(solution)/shard_map/ppermute | solution.py:17
  130.3 4.8 %copy.131 = bf16[1,1,256,2048]{3,1,0,2:T(2,128)(2,1)S(1)} copy(bf16[1,1,256,2048]{2,3,1,0:T(8,128)(2,1)} %bitcast.315) | data formatting | bytes 2097152 | tf_op jit(solution)/shard_map/convert_element_type | solution.py:130
  135.0 6.8 %reduce.4 = bf16[256,2048]{1,0:T(8,128)(2,1)S(1)} reduce(bf16[256,1,1,2048]{3,2,1,0:T(2,128)(2,1)S(1)} %bitcast.307, bf16[]{:T(256)} %broadcast.60), dimensions={1,2}, to_apply=%bitcast.205.reduce_sub_computation | reduce | bytes 2097154
  141.9 1.6 reshape.113
  143.5 3.7 %all-to-all-start.2 = ((bf16[2,2,131072]{2,1,0:T(2,128)(2,1)}), bf16[2,2,131072]{2,1,0:T(2,128)(2,1)S(1)}, u32[]{:S(2)}, u32[]{:S(2)}) async-start(bf16[2,2,131072]{2,1,0:T(2,128)(2,1)} %reshape.113), calls=%async_computation.2 | async-start | bytes 2097152 | tf_op jit(solution)/shard_map/all_to_all | solution.py:131
  147.4 1.9 %collective-permute-start.5 = (bf16[1,1,256,256]{3,2,1,0:T(8,128)(2,1)S(1)}, bf16[1,1,256,256]{3,2,1,0:T(8,128)(2,1)S(1)}, u32[]{:S(2)}, u32[]{:S(2)}) collective-permute-start(bf16[1,1,256,256]{3,2,1,0:T(8,128)(2,1)S(1)} %convert_element_type.101), channel_id=1, source_target_pairs={{4,0},{8,4},{12,8},{5,1},{9,5},{13,9},{6,2},{10,6},{14,10},{7,3},{... | collective-permute-start | bytes 393224 | tf_op jit(solution)/shard_map/ppermute | solution.py:17
  150.3 0.7 add_convert_fusion.1
  151.0 3.1 %collective-permute-done.5 = bf16[1,1,256,256]{3,2,1,0:T(8,128)(2,1)S(1)} collective-permute-done((bf16[1,1,256,256]{3,2,1,0:T(8,128)(2,1)S(1)}, bf16[1,1,256,256]{3,2,1,0:T(8,128)(2,1)S(1)}, u32[]{:S(2)}, u32[]{:S(2)}) %collective-permute-start.5) | collective-permute-done | bytes 131104 | tf_op jit(solution)/shard_map/ppermute | solution.py:17
  154.0 0.7 add_convert_fusion
  154.7 6.3 %all-to-all-done.2 = bf16[2,2,131072]{2,1,0:T(2,128)(2,1)S(1)} async-done(((bf16[2,2,131072]{2,1,0:T(2,128)(2,1)}), bf16[2,2,131072]{2,1,0:T(2,128)(2,1)S(1)}, u32[]{:S(2)}, u32[]{:S(2)}) %all-to-all-start.2) | async-done | bytes 1048608 | tf_op jit(solution)/shard_map/all_to_all | solution.py:131
  161.0 0.9 reshape.114
  163.2 1.3 copy.137
  (121 shorter events, 17.2 us)
Async XLA Ops:
  1.3 79.8 %collective-permute-start.3 = (bf16[1,1,2,2]{3,2,1,0:T(2,128)(2,1)S(1)}, bf16[1,1,2,2]{3,2,1,0:T(2,128)(2,1)S(1)}, u32[]{:S(2)}, u32[]{:S(2)}) collective-permute-start(bf16[1,1,2,2]{3,2,1,0:T(2,128)(2,1)S(1)} %exponential_convert_fusion), channel_id=1, source_target_pairs={{0,4},{4,8},{8,12},{1,5},{5,9},{9,13},{2,6},{6,10},{10,14},{3,7},{... | collective-permute-start | bytes 32 | tf_op jit(solution)/shard_map/ppermute | solution.py:17
  6.5 74.7 %collective-permute-start.1 = (bf16[1,1,2,2]{3,2,1,0:T(2,128)(2,1)S(1)}, bf16[1,1,2,2]{3,2,1,0:T(2,128)(2,1)S(1)}, u32[]{:S(2)}, u32[]{:S(2)}) collective-permute-start(bf16[1,1,2,2]{3,2,1,0:T(2,128)(2,1)S(1)} %exponential_convert_fusion.1), channel_id=1, source_target_pairs={{0,4},{4,8},{8,12},{1,5},{5,9},{9,13},{2,6},{6,10},{10,14},{3,7},{... | collective-permute-start | bytes 32 | tf_op jit(solution)/shard_map/ppermute | solution.py:17
  10.1 76.1 %collective-permute-start.2 = (bf16[1,1,256,256]{2,3,1,0:T(8,128)(2,1)}, bf16[1,1,256,256]{2,3,1,0:T(8,128)(2,1)}, u32[]{:S(2)}, u32[]{:S(2)}) collective-permute-start(bf16[1,1,256,256]{2,3,1,0:T(8,128)(2,1)} %copy.119), channel_id=1, source_target_pairs={{0,4},{4,8},{8,12},{1,5},{5,9},{9,13},{2,6},{6,10},{10,14},{3,7},{... | collective-permute-start | bytes 393224 | tf_op jit(solution)/shard_map/ppermute | solution.py:17
  13.7 74.1 %collective-permute-start = (bf16[1,1,256,256]{2,3,1,0:T(8,128)(2,1)}, bf16[1,1,256,256]{2,3,1,0:T(8,128)(2,1)}, u32[]{:S(2)}, u32[]{:S(2)}) collective-permute-start(bf16[1,1,256,256]{2,3,1,0:T(8,128)(2,1)} %copy.113), channel_id=1, source_target_pairs={{0,4},{4,8},{8,12},{1,5},{5,9},{9,13},{2,6},{6,10},{10,14},{3,7},{... | collective-permute-start | bytes 393224 | tf_op jit(solution)/shard_map/ppermute | solution.py:17
  43.6 4.8 %copy-start.14 = (s32[1,1,2,2]{3,2,1,0:T(2,128)S(1)}, s32[1,1,2,2]{3,2,1,0:T(2,128)}, u32[]{:S(2)}) copy-start(s32[1,1,2,2]{3,2,1,0:T(2,128)} %param.13) | copy-start | bytes 52
  43.6 4.8 %copy-start.15 = (s32[1,1,2,2]{3,2,1,0:T(2,128)S(1)}, s32[1,1,2,2]{3,2,1,0:T(2,128)}, u32[]{:S(2)}) copy-start(s32[1,1,2,2]{3,2,1,0:T(2,128)} %param.14) | copy-start | bytes 52
  44.8 36.6 %all-to-all-start = ((bf16[2,2,131072]{2,1,0:T(2,128)(2,1)}), bf16[2,2,131072]{2,1,0:T(2,128)(2,1)S(1)}, u32[]{:S(2)}, u32[]{:S(2)}) async-start(bf16[2,2,131072]{2,1,0:T(2,128)(2,1)} %reshape.109), calls=%async_computation | async-start | bytes 2097152 | tf_op jit(solution)/shard_map/all_to_all | solution.py:116
  81.4 17.1 %all-to-all-start.1 = ((bf16[2,2,131072]{2,1,0:T(2,128)(2,1)}), bf16[2,2,131072]{2,1,0:T(2,128)(2,1)}, u32[]{:S(2)}, u32[]{:S(2)}) async-start(bf16[2,2,131072]{2,1,0:T(2,128)(2,1)} %reshape.111), calls=%async_computation.1 | async-start | bytes 2097152 | tf_op jit(solution)/shard_map/all_to_all | solution.py:117
  104.6 0.9 copy-start.9
  106.3 1.4 copy-start.10
  106.3 1.0 copy-start.2
  107.3 0.9 copy-start.8
  107.7 1.5 copy-start.3
  110.2 0.9 copy-start.12
  110.2 1.4 copy-start.5
  111.5 1.6 copy-start.13
  111.5 1.3 copy-start
  112.0 1.2 copy-start.6
  113.2 1.0 copy-start.1
  115.3 0.9 copy-start.9
  117.0 1.4 copy-start.10
  117.0 1.0 copy-start.2
  118.0 0.9 copy-start.8
  118.5 1.5 copy-start.3
  120.9 0.9 copy-start.12
  120.9 1.4 copy-start.5
  122.3 1.6 copy-start.13
  122.3 1.3 copy-start
  122.8 1.1 copy-start.6
  123.9 1.0 copy-start.1
  126.0 24.2 %collective-permute-start.4 = (bf16[1,1,256,256]{3,2,1,0:T(8,128)(2,1)S(1)}, bf16[1,1,256,256]{3,2,1,0:T(8,128)(2,1)S(1)}, u32[]{:S(2)}, u32[]{:S(2)}) collective-permute-start(bf16[1,1,256,256]{3,2,1,0:T(8,128)(2,1)S(1)} %convert_element_type.96), channel_id=1, source_target_pairs={{4,0},{8,4},{12,8},{5,1},{9,5},{13,9},{6,2},{10,6},{14,10},{7,3},{... | collective-permute-start | bytes 393224 | tf_op jit(solution)/shard_map/ppermute | solution.py:17
  141.9 5.3 %copy-start.11 = (bf16[2,256,128]{2,1,0:T(8,128)(2,1)S(1)}, bf16[2,256,128]{2,1,0:T(8,128)(2,1)}, u32[]{:S(2)}) copy-start(bf16[2,256,128]{2,1,0:T(8,128)(2,1)} %get-tuple-element.83) | copy-start | bytes 393220
  141.9 7.5 %copy-start.7 = (f32[2,256,128]{2,1,0:T(8,128)S(1)}, f32[2,256,128]{2,1,0:T(8,128)}, u32[]{:S(2)}) copy-start(f32[2,256,128]{2,1,0:T(8,128)} %get-tuple-element.80) | copy-start | bytes 786436
  143.5 6.3 %copy-start.4 = (f32[2,256,128]{2,1,0:T(8,128)S(1)}, f32[2,256,128]{2,1,0:T(8,128)}, u32[]{:S(2)}) copy-start(f32[2,256,128]{2,1,0:T(8,128)} %get-tuple-element.82) | copy-start | bytes 786436
  143.5 17.5 %all-to-all-start.2 = ((bf16[2,2,131072]{2,1,0:T(2,128)(2,1)}), bf16[2,2,131072]{2,1,0:T(2,128)(2,1)S(1)}, u32[]{:S(2)}, u32[]{:S(2)}) async-start(bf16[2,2,131072]{2,1,0:T(2,128)(2,1)} %reshape.113), calls=%async_computation.2 | async-start | bytes 2097152 | tf_op jit(solution)/shard_map/all_to_all | solution.py:131
  147.4 6.6 %collective-permute-start.5 = (bf16[1,1,256,256]{3,2,1,0:T(8,128)(2,1)S(1)}, bf16[1,1,256,256]{3,2,1,0:T(8,128)(2,1)S(1)}, u32[]{:S(2)}, u32[]{:S(2)}) collective-permute-start(bf16[1,1,256,256]{3,2,1,0:T(8,128)(2,1)S(1)} %convert_element_type.101), channel_id=1, source_target_pairs={{4,0},{8,4},{12,8},{5,1},{9,5},{13,9},{6,2},{10,6},{14,10},{7,3},{... | collective-permute-start | bytes 393224 | tf_op jit(solution)/shard_map/ppermute | solution.py:17
where the time goes:
time: 166 us; the launch traced here: 165 us
  other arithmetic  61.2 us (37%)
  local copies, waits for them, and re-layouts  41.8 us (25%)
  starting transfers between devices  28.3 us (17%)
  waiting for transfers between devices  17.4 us (10%)
  matrix products  13.6 us (8%)
  between operations  1.67 us (1%)
    unnamed x3, other arithmetic  52.7 us
    unnamed x35, local copies, waits for them, and re-layouts  26.6 us
    ppermute x6, starting transfers between devices, passed_along(): lax.ppermute(value, axis, [(source, source + steps) for source in range(i...  16.4 us
    all_to_all x1, waiting for transfers between devices, on_device(): lax.all_to_all(dout, 'head', split_axis=3, concat_axis=2, tiled=True)  8.04 us
    all_to_all x1, waiting for transfers between devices, on_device(): lax.all_to_all(rounded, 'head', split_axis=2, concat_axis=3, tiled=True)  6.31 us
    while x44, local copies, waits for them, and re-layouts  4.99 us
    convert_element_type x1, local copies, waits for them, and re-layouts, on_device(): rounded = query_grad.astype(jnp.bfloat16).reshape(1, 1, length, -1)  4.75 us
    all_to_all x1, starting transfers between devices, on_device(): lax.all_to_all(dout, 'head', split_axis=3, concat_axis=2, tiled=True)  4.64 us
  transfers between devices with their start and end apart: 9, of which 3 were waited for; matrix products, arithmetic and copies ran while one was open for 52% of the time, Pallas kernels for 0%

commit v1 on v0

v1 whole, which is shorter than its diff:
```python
import functools

import jax
import jax.numpy as jnp
from jax import lax
from jax.experimental import pallas as pl
from jax.experimental.pallas import tpu as pltpu
from jax.sharding import PartitionSpec as P

D = 128
GROUP = 8
LOG2E = 1.4426950408889634
NEG_FILL = -1e30
F32 = jnp.float32
BF16 = jnp.bfloat16
MESH = pl.DeviceIdType.MESH


def scale_of(exponent):
    return jnp.where(exponent > 0, 2.0, jnp.where(exponent < 0, 0.5, 1.0)).astype(F32)


def kernel(
    ring,
    q_hbm,
    do_hbm,
    km_ref,
    vm_ref,
    ke_ref,
    ve_ref,
    reach_ref,
    dq_hbm,
    dk_ref,
    dv_ref,
    q_s,
    do_s,
    dq_s,
    kv,
    bias,
    p_s,
    ds_s,
    own,
    gsend,
    grecv,
    fsend,
    frecv,
    q_sem,
    do_sem,
    dq_sem,
    a_send,
    a_recv,
    b_send,
    b_recv,
    d_send,
    d_recv,
    f_send,
    f_recv,
):
    rows = q_s.shape[1]
    length = km_ref.shape[2]
    width = q_s.shape[2]
    mine = km_ref.shape[3] // D
    heads = 2 * mine
    factor = D**-0.5

    h = lax.axis_index("head")
    r = lax.axis_index("inner")
    other = 1 - h
    has_prev = r > 0
    has_next = r < ring - 1

    def columns(slot):
        return pl.ds(pl.multiple_of(lax.rem(mine * h + slot, heads) * width, width), width)

    def load_q(slot):
        return pltpu.make_async_copy(q_hbm.at[0, 0, :, columns(slot)], q_s.at[slot], q_sem.at[slot])

    def load_do(slot):
        return pltpu.make_async_copy(
            do_hbm.at[0, 0, :, columns(slot)], do_s.at[slot], do_sem.at[slot]
        )

    def store_dq(slot):
        return pltpu.make_async_copy(
            dq_s.at[slot], dq_hbm.at[0, 0, :, columns(slot)], dq_sem.at[slot]
        )

    def copy_a(j):
        return pltpu.make_async_remote_copy(
            src_ref=kv.at[j, :, pl.ds(length, length)],
            dst_ref=kv.at[mine + j, :, pl.ds(length, length)],
            send_sem=a_send.at[j],
            recv_sem=a_recv.at[j],
            device_id={"head": other},
            device_id_type=MESH,
        )

    def copy_b(slot):
        return pltpu.make_async_remote_copy(
            src_ref=kv.at[slot, :, pl.ds(length, length)],
            dst_ref=kv.at[slot, :, pl.ds(0, length)],
            send_sem=b_send.at[slot],
            recv_sem=b_recv.at[slot],
            device_id={"inner": r + 1},
            device_id_type=MESH,
        )

    def copy_d(slot):
        return pltpu.make_async_remote_copy(
            src_ref=gsend.at[slot],
            dst_ref=grecv.at[slot],
            send_sem=d_send.at[slot],
            recv_sem=d_recv.at[slot],
            device_id={"inner": r - 1},
            device_id_type=MESH,
        )

    def copy_f(j):
        return pltpu.make_async_remote_copy(
            src_ref=fsend.at[j],
            dst_ref=frecv.at[j],
            send_sem=f_send.at[j],
            recv_sem=f_recv.at[j],
            device_id={"head": other},
            device_id_type=MESH,
        )

    barrier = pltpu.get_barrier_semaphore()
    pl.semaphore_signal(barrier, inc=1, device_id={"head": other}, device_id_type=MESH)

    @pl.when(has_prev)
    def _():
        pl.semaphore_signal(barrier, inc=1, device_id={"inner": r - 1}, device_id_type=MESH)

    @pl.when(has_next)
    def _():
        pl.semaphore_signal(barrier, inc=1, device_id={"inner": r + 1}, device_id_type=MESH)

    for slot in range(heads):
        load_q(slot).start()
        load_do(slot).start()

    half = length // 2
    for j in range(mine):
        for b in range(2):
            for which, mant, exps in ((0, km_ref, ke_ref), (1, vm_ref, ve_ref)):
                block = mant[0, 0, b * half : (b + 1) * half, j * D : (j + 1) * D].astype(F32)
                kv[j, which, length + b * half : length + (b + 1) * half, :] = (
                    block * scale_of(exps[0, 0, b, j])
                ).astype(BF16)

    pl.semaphore_wait(barrier, 1 + has_prev.astype(jnp.int32) + has_next.astype(jnp.int32))

    for j in range(mine):
        copy_a(j).start()

        @pl.when(has_next)
        def _():
            copy_b(j).start()

    key_at = lax.broadcasted_iota(jnp.int32, (length, 2 * rows), 0)
    query_at = lax.rem(lax.broadcasted_iota(jnp.int32, (length, 2 * rows), 1), rows) + h * rows
    first_seen = jnp.where(has_prev, length - reach_ref[0, 0], length)
    bias[0:length, :] = jnp.where(key_at >= first_seen, 0.0, NEG_FILL).astype(F32)
    bias[length : 2 * length, :] = jnp.where(key_at <= query_at, 0.0, NEG_FILL).astype(F32)

    @pl.when(jnp.logical_not(has_prev))
    def _():
        for slot in range(heads):
            kv[slot, :, 0:length, :] = jnp.zeros((2, length, D), BF16)

    @pl.when(jnp.logical_not(has_next))
    def _():
        grecv[...] = jnp.zeros_like(grecv)

    def finish(j):
        @pl.when(has_next)
        def _():
            copy_d(mine + j).wait_recv()

        fsend[j] = (own[mine + j] + grecv[mine + j].astype(F32)).astype(BF16)
        copy_f(j).start()

    def one_slot(slot, carry):
        load_q(slot).wait()
        load_do(slot).wait()

        for j in range(mine):
            @pl.when(slot == j + 1)
            def _():
                copy_a(j).wait_recv()

                @pl.when(has_next)
                def _():
                    copy_b(mine + j).start()

        @pl.when(has_prev)
        def _():
            copy_b(slot).wait_recv()

        keys = kv[slot, 0]
        values = kv[slot, 1]
        keys_t = keys.T
        q_list, do_list = [], []
        for pair in range(GROUP // 2):
            at = pair * 2 * D
            q_pair = jnp.concatenate(
                [q_s[slot, :, at : at + D], q_s[slot, :, at + D : at + 2 * D]], axis=0
            )
            do_pair = jnp.concatenate(
                [do_s[slot, :, at : at + D], do_s[slot, :, at + D : at + 2 * D]], axis=0
            )
            q_list.append(q_pair)
            do_list.append(do_pair)
            contract = (((1,), (1,)), ((), ()))
            scores = lax.dot_general(keys, q_pair, contract, preferred_element_type=F32)
            scores = scores * (factor * LOG2E) + bias[...]
            peak = jnp.max(scores, axis=0, keepdims=True)
            weights = jnp.exp2(scores - peak)
            total = jnp.sum(weights, axis=0, keepdims=True)
            probs = weights * (1.0 / total)
            rounded = probs.astype(BF16)
            dprob = lax.dot_general(values, do_pair, contract, preferred_element_type=F32)
            row_dot = jnp.sum(rounded.astype(F32) * dprob, axis=0, keepdims=True)
            dscore = (probs * (dprob - row_dot)).astype(BF16)
            span = slice(pair * 2 * rows, (pair + 1) * 2 * rows)
            p_s[:, span] = rounded
            ds_s[:, span] = dscore
            grad_t = jnp.dot(keys_t, dscore, preferred_element_type=F32) * factor
            dq_s[slot, :, at : at + D] = grad_t[:, :rows].T.astype(BF16)
            dq_s[slot, :, at + D : at + 2 * D] = grad_t[:, rows:].T.astype(BF16)
        store_dq(slot).start()

        @pl.when(slot == mine + 1)
        def _():
            finish(0)

        dv = jnp.dot(p_s[...], jnp.concatenate(do_list, axis=0), preferred_element_type=F32)
        dk = jnp.dot(ds_s[...], jnp.concatenate(q_list, axis=0), preferred_element_type=F32) * factor
        gsend[slot, 0] = dk[:length].astype(BF16)
        gsend[slot, 1] = dv[:length].astype(BF16)

        @pl.when(has_prev)
        def _():
            copy_d(slot).start()

        own[slot, 0] = dk[length:]
        own[slot, 1] = dv[length:]
        return carry

    lax.fori_loop(0, heads, one_slot, 0)
    for j in range(1, mine):
        finish(j)

    for j in range(mine):

        @pl.when(has_next)
        def _():
            copy_d(j).wait_recv()

        copy_f(j).wait_recv()
        total = own[j] + grecv[j].astype(F32) + frecv[j].astype(F32)
        dk_ref[0, 0, :, j * D : (j + 1) * D] = total[0].astype(BF16)
        dv_ref[0, 0, :, j * D : (j + 1) * D] = total[1].astype(BF16)

    for j in range(mine):
        copy_a(j).wait_send()
        copy_f(j).wait_send()
    for slot in range(heads):
        store_dq(slot).wait()

        @pl.when(has_next)
        def _():
            copy_b(slot).wait_send()

        @pl.when(has_prev)
        def _():
            copy_d(slot).wait_send()


def on_device(ring, query, dout, key_mant, value_mantissas, key_exps, value_exponents, reach):
    rows, length = query.shape[2], key_mant.shape[2]
    mine = key_mant.shape[3] // D
    heads = 2 * mine
    width = GROUP * D
    hbm = pl.BlockSpec(memory_space=pl.ANY)
    vmem = pl.BlockSpec(memory_space=pltpu.VMEM)
    smem = pl.BlockSpec(memory_space=pltpu.SMEM)
    dma = pltpu.SemaphoreType.DMA
    return pl.pallas_call(
        functools.partial(kernel, ring),
        out_shape=(
            jax.ShapeDtypeStruct(query.shape, BF16),
            jax.ShapeDtypeStruct(key_mant.shape, BF16),
            jax.ShapeDtypeStruct(key_mant.shape, BF16),
        ),
        in_specs=[hbm, hbm, vmem, vmem, smem, smem, smem],
        out_specs=(hbm, vmem, vmem),
        scratch_shapes=[
            pltpu.VMEM((heads, rows, width), BF16),
            pltpu.VMEM((heads, rows, width), BF16),
            pltpu.VMEM((heads, rows, width), BF16),
            pltpu.VMEM((heads, 2, 2 * length, D), BF16),
            pltpu.VMEM((2 * length, 2 * rows), F32),
            pltpu.VMEM((2 * length, GROUP * rows), BF16),
            pltpu.VMEM((2 * length, GROUP * rows), BF16),
            pltpu.VMEM((heads, 2, length, D), F32),
            pltpu.VMEM((heads, 2, length, D), BF16),
            pltpu.VMEM((heads, 2, length, D), BF16),
            pltpu.VMEM((mine, 2, length, D), BF16),
            pltpu.VMEM((mine, 2, length, D), BF16),
            dma((heads,)),
            dma((heads,)),
            dma((heads,)),
            dma((mine,)),
            dma((mine,)),
            dma((heads,)),
            dma((heads,)),
            dma((heads,)),
            dma((heads,)),
            dma((mine,)),
            dma((mine,)),
        ],
        compiler_params=pltpu.CompilerParams(
            collective_id=0, has_side_effects=True, vmem_limit_bytes=48 * 2**20
        ),
        cost_estimate=pl.CostEstimate(
            flops=10 * heads * width * rows * 2 * length,
            bytes_accessed=6 * rows * heads * width,
            transcendentals=heads * GROUP * rows * 2 * length,
        ),
    )(query, dout, key_mant, value_mantissas, key_exps, value_exponents, reach)


def solution(mesh):
    assert mesh.shape["head"] == 2
    tokens = P("outer", "inner", "head", None)
    shared = P("outer", "inner", None, "head")
    return jax.shard_map(
        functools.partial(on_device, mesh.shape["inner"]),
        mesh=mesh,
        in_specs=(tokens, tokens, shared, shared, shared, shared, P("outer", "inner")),
        out_specs=(tokens, shared, shared),
        check_vma=False,
    )
```

time: 166 us -> 35.6 us (0.21)
  other arithmetic: 61.2 us -> 0 us
  local copies, waits for them, and re-layouts: 41.8 us -> 7.22 us
  starting transfers between devices: 28.3 us -> 0 us
  Pallas kernels: 0 us -> 26.8 us
  waiting for transfers between devices: 17.4 us -> 0 us
  matrix products: 13.6 us -> 0 us
    unnamed x3 -> x0, other arithmetic: 52.7 us -> none
    pallas_call x0 -> x1, Pallas kernels: none -> 26.8 us  [on_device(): pl.pallas_call(functools.partial(kernel, ring), out_shape=(jax.ShapeDtype...]
    unnamed x35 -> x15, local copies, waits for them, and re-layouts: 26.6 us -> 7.22 us
    ppermute x6 -> x0, starting transfers between devices: 16.4 us -> none  [passed_along(): lax.ppermute(value, axis, [(source, source + steps) for source in range(i...]
    all_to_all x3 -> x0, waiting for transfers between devices: 14.3 us -> none  [the longest x1 8.04 us: on_device(): lax.all_to_all(dout, 'head', split_axis=3, concat_axis=2, tiled=True)]
    dot_general x24 -> x0, matrix products: 13.6 us -> none  [the longest x2 2.03 us: per_head(): jnp.einsum('gts,sd->gtd', rounded_prev, value_prev, preferred_element_typ...]
    all_to_all x3 -> x0, starting transfers between devices: 11.9 us -> none  [the longest x1 4.64 us: on_device(): lax.all_to_all(dout, 'head', split_axis=3, concat_axis=2, tiled=True)]
    convert_element_type x5 -> x0, local copies, waits for them, and re-layouts: 6.11 us -> none  [the longest x1 4.75 us: on_device(): rounded = query_grad.astype(jnp.bfloat16).reshape(1, 1, length, -1)]
  transfers between devices with their start and end apart: 9 -> 0, of which waited for: 3 -> 0; matrix products, arithmetic and copies ran while one was open for 52% -> 0% of each run, Pallas kernels for 0% -> 0%
where the time goes in v1:
time: 35.6 us; the launch traced here: 35.4 us
  Pallas kernels  26.8 us (75%)
  local copies, waits for them, and re-layouts  7.22 us (20%)
  between operations  1.32 us (4%)
    pallas_call x1, Pallas kernels, on_device(): pl.pallas_call(functools.partial(kernel, ring), out_shape=(jax.ShapeDtype...  26.8 us
    unnamed x15, local copies, waits for them, and re-layouts  7.22 us

profile of v1, /device:TPU:1, one launch (start us, length us, event | category | flops | bytes accessed | tf_op | source)
XLA Modules:
  0.0 35.4 jit_solution(4977798120706681746)
XLA Ops:
  0.6 0.0 copy-start.4
  1.3 0.0 copy-done.4
  1.3 0.0 copy-start
  1.3 1.2 %copy-done = bf16[1,1,128,4096]{3,2,1,0:T(8,128)(2,1)S(1)} copy-done((bf16[1,1,128,4096]{3,2,1,0:T(8,128)(2,1)S(1)}, bf16[1,1,128,4096]{3,2,1,0:T(8,128)(2,1)}, u32[]{:S(2)}) %copy-start) | copy-done | bytes 1048600
  2.5 0.0 copy-start.1
  2.5 1.2 %copy-done.1 = bf16[1,1,128,4096]{3,2,1,0:T(8,128)(2,1)S(1)} copy-done((bf16[1,1,128,4096]{3,2,1,0:T(8,128)(2,1)S(1)}, bf16[1,1,128,4096]{3,2,1,0:T(8,128)(2,1)}, u32[]{:S(2)}) %copy-start.1) | copy-done | bytes 1048600
  3.8 0.0 copy-start.2
  3.8 0.9 %copy-done.2 = bf16[1,1,256,256]{3,2,1,0:T(8,128)(2,1)S(1)} copy-done((bf16[1,1,256,256]{3,2,1,0:T(8,128)(2,1)S(1)}, bf16[1,1,256,256]{3,2,1,0:T(8,128)(2,1)}, u32[]{:S(2)}) %copy-start.2) | copy-done | bytes 131096
  4.7 0.0 copy-start.3
  4.7 0.9 %copy-done.3 = bf16[1,1,256,256]{3,2,1,0:T(8,128)(2,1)S(1)} copy-done((bf16[1,1,256,256]{3,2,1,0:T(8,128)(2,1)S(1)}, bf16[1,1,256,256]{3,2,1,0:T(8,128)(2,1)}, u32[]{:S(2)}) %copy-start.3) | copy-done | bytes 131096
  5.6 0.0 copy-start.5
  5.6 0.7 %copy-done.5 = s32[1,1,2,2]{3,2,1,0:T(2,128)S(1)} copy-done((s32[1,1,2,2]{3,2,1,0:T(2,128)S(1)}, s32[1,1,2,2]{3,2,1,0:T(2,128)}, u32[]{:S(2)}) %copy-start.5) | copy-done | bytes 40
  6.3 26.8 %shard_map.94 = (bf16[1,1,128,4096]{3,2,1,0:T(8,128)(2,1)S(1)}, bf16[1,1,256,256]{3,2,1,0:T(8,128)(2,1)S(1)}, bf16[1,1,256,256]{3,2,1,0:T(8,128)(2,1)S(1)}) custom-call(bf16[1,1,128,4096]{3,2,1,0:T(8,128)(2,1)S(1)} %copy-done, bf16[1,1,128,4096]{3,2,1,0:T(8,128)(2,1)S(1)} %copy-done.1, bf16[1,1,256,256]{3,2,1,0:T(8,128)(2,1)S(1)} %copy-done.2, ...), custom_call_target="tpu_custom_call" | custom-call | flops 2684354560 | bytes 3145728 | tf_op jit(solution)/shard_map/pallas_call | solution.py:290
  33.1 1.0 %copy.14 = bf16[1,1,128,4096]{3,2,1,0:T(8,128)(2,1)} copy(bf16[1,1,128,4096]{3,2,1,0:T(8,128)(2,1)S(1)} %get-tuple-element.6) | data formatting | bytes 2097152
  34.1 0.7 %copy.15 = bf16[1,1,256,256]{3,2,1,0:T(8,128)(2,1)} copy(bf16[1,1,256,256]{3,2,1,0:T(8,128)(2,1)S(1)} %get-tuple-element.7) | data formatting | bytes 262144
  34.7 0.7 %copy.16 = bf16[1,1,256,256]{3,2,1,0:T(8,128)(2,1)} copy(bf16[1,1,256,256]{3,2,1,0:T(8,128)(2,1)S(1)} %get-tuple-element.8) | data formatting | bytes 262144
Async XLA Ops:
  0.6 0.7 %copy-start.4 = (s32[1,1,2,2]{3,2,1,0:T(2,128)S(1)}, s32[1,1,2,2]{3,2,1,0:T(2,128)}, u32[]{:S(2)}) copy-start(s32[1,1,2,2]{3,2,1,0:T(2,128)} %ke_ref.1) | copy-start | bytes 52
  1.3 1.2 %copy-start = (bf16[1,1,128,4096]{3,2,1,0:T(8,128)(2,1)S(1)}, bf16[1,1,128,4096]{3,2,1,0:T(8,128)(2,1)}, u32[]{:S(2)}) copy-start(bf16[1,1,128,4096]{3,2,1,0:T(8,128)(2,1)} %q_hbm.1) | copy-start | bytes 3145732
  2.5 1.2 %copy-start.1 = (bf16[1,1,128,4096]{3,2,1,0:T(8,128)(2,1)S(1)}, bf16[1,1,128,4096]{3,2,1,0:T(8,128)(2,1)}, u32[]{:S(2)}) copy-start(bf16[1,1,128,4096]{3,2,1,0:T(8,128)(2,1)} %do_hbm.1) | copy-start | bytes 3145732
  3.8 0.9 %copy-start.2 = (bf16[1,1,256,256]{3,2,1,0:T(8,128)(2,1)S(1)}, bf16[1,1,256,256]{3,2,1,0:T(8,128)(2,1)}, u32[]{:S(2)}) copy-start(bf16[1,1,256,256]{3,2,1,0:T(8,128)(2,1)} %km_ref.1) | copy-start | bytes 393220
  4.7 0.9 %copy-start.3 = (bf16[1,1,256,256]{3,2,1,0:T(8,128)(2,1)S(1)}, bf16[1,1,256,256]{3,2,1,0:T(8,128)(2,1)}, u32[]{:S(2)}) copy-start(bf16[1,1,256,256]{3,2,1,0:T(8,128)(2,1)} %vm_ref.1) | copy-start | bytes 393220
  5.6 0.7 %copy-start.5 = (s32[1,1,2,2]{3,2,1,0:T(2,128)S(1)}, s32[1,1,2,2]{3,2,1,0:T(2,128)}, u32[]{:S(2)}) copy-start(s32[1,1,2,2]{3,2,1,0:T(2,128)} %ve_ref.1) | copy-start | bytes 52

commit v2 on v1

--- a/solution.py
+++ b/solution.py
@@ -24,19 +24,25 @@
     ring,
     q_hbm,
     do_hbm,
+    km_hbm,
+    vm_hbm,
+    ke_hbm,
+    ve_hbm,
+    reach_hbm,
+    dq_ref,
+    dk_ref,
+    dv_ref,
+    q_s,
+    do_s,
     km_ref,
     vm_ref,
     ke_ref,
     ve_ref,
     reach_ref,
-    dq_hbm,
-    dk_ref,
-    dv_ref,
-    q_s,
-    do_s,
-    dq_s,
     kv,
     bias,
+    s_buf,
+    dp_buf,
     p_s,
     ds_s,
     own,
@@ -44,9 +50,10 @@
     grecv,
     fsend,
     frecv,
+    part,
+    in_sem,
     q_sem,
     do_sem,
-    dq_sem,
     a_send,
     a_recv,
     b_send,
@@ -80,11 +87,6 @@
             do_hbm.at[0, 0, :, columns(slot)], do_s.at[slot], do_sem.at[slot]
         )
 
-    def store_dq(slot):
-        return pltpu.make_async_copy(
-            dq_s.at[slot], dq_hbm.at[0, 0, :, columns(slot)], dq_sem.at[slot]
-        )
-
     def copy_a(j):
         return pltpu.make_async_remote_copy(
             src_ref=kv.at[j, :, pl.ds(length, length)],
@@ -136,9 +138,25 @@
     def _():
         pl.semaphore_signal(barrier, inc=1, device_id={"inner": r + 1}, device_id_type=MESH)
 
+    small = [
+        pltpu.make_async_copy(source, target, in_sem.at[n])
+        for n, (source, target) in enumerate(
+            (
+                (ke_hbm, ke_ref),
+                (ve_hbm, ve_ref),
+                (km_hbm, km_ref),
+                (vm_hbm, vm_ref),
+                (reach_hbm, reach_ref),
+            )
+        )
+    ]
+    for copy in small:
+        copy.start()
     for slot in range(heads):
         load_q(slot).start()
         load_do(slot).start()
+    for copy in small:
+        copy.wait()
 
     half = length // 2
     for j in range(mine):
@@ -152,11 +170,12 @@
     pl.semaphore_wait(barrier, 1 + has_prev.astype(jnp.int32) + has_next.astype(jnp.int32))
 
     for j in range(mine):
+
+        @pl.when(has_next)
+        def _():
+            copy_b(j).start()
+
         copy_a(j).start()
-
-        @pl.when(has_next)
-        def _():
-            copy_b(j).start()
 
     key_at = lax.broadcasted_iota(jnp.int32, (length, 2 * rows), 0)
     query_at = lax.rem(lax.broadcasted_iota(jnp.int32, (length, 2 * rows), 1), rows) + h * rows
@@ -173,6 +192,13 @@
     def _():
         grecv[...] = jnp.zeros_like(grecv)
 
+    def pass_on(j):
+        copy_a(j).wait_recv()
+
+        @pl.when(has_next)
+        def _():
+            copy_b(mine + j).start()
+
     def finish(j):
         @pl.when(has_next)
         def _():
@@ -181,76 +207,153 @@
         fsend[j] = (own[mine + j] + grecv[mine + j].astype(F32)).astype(BF16)
         copy_f(j).start()
 
-    def one_slot(slot, carry):
+    chunk = 64
+    chunks = 2 * length // chunk
+    wide = 2 * rows
+    contract = (((1,), (1,)), ((), ()))
+
+    def fold(x, op):
+        folded = x[0:8]
+        for at in range(8, chunk, 8):
+            folded = op(folded, x[at : at + 8])
+        return folded
+
+    def softmax(pair):
+        here = pair % 2
+        span = slice(pair * wide, (pair + 1) * wide)
+        peak = None
+        for c in range(chunks):
+            at = slice(c * chunk, (c + 1) * chunk)
+            x = s_buf[here, at] * (factor * LOG2E) + bias[at]
+            s_buf[here, at] = x
+            top = fold(x, jnp.maximum)
+            peak = top if peak is None else jnp.maximum(peak, top)
+        peak = jnp.max(peak, axis=0, keepdims=True)
+        total = None
+        for c in range(chunks):
+            at = slice(c * chunk, (c + 1) * chunk)
+            x = jnp.exp2(s_buf[here, at] - peak)
+            s_buf[here, at] = x
+            some = fold(x, jnp.add)
+            total = some if total is None else total + some
+        inverse = 1.0 / jnp.sum(total, axis=0, keepdims=True)
+        row_dot = None
+        for c in range(chunks):
+            at = slice(c * chunk, (c + 1) * chunk)
+            rounded = (s_buf[here, at] * inverse).astype(BF16)
+            p_s[at, span] = rounded
+            some = fold(rounded.astype(F32) * dp_buf[here, at], jnp.add)
+            row_dot = some if row_dot is None else row_dot + some
+        row_dot = jnp.sum(row_dot, axis=0, keepdims=True)
+        for c in range(chunks):
+            at = slice(c * chunk, (c + 1) * chunk)
+            x = (s_buf[here, at] * inverse) * (dp_buf[here, at] - row_dot)
+            ds_s[at, span] = x.astype(BF16)
+
+    def one_step(step, carry):
+        slot = step + (step + heads - 2) // (heads - 1) - (heads - 1) * (step // (heads - 1))
         load_q(slot).wait()
         load_do(slot).wait()
 
-        for j in range(mine):
-            @pl.when(slot == j + 1)
-            def _():
-                copy_a(j).wait_recv()
-
-                @pl.when(has_next)
-                def _():
-                    copy_b(mine + j).start()
+        @pl.when(step == 1)
+        def _():
+            pass_on(1)
 
         @pl.when(has_prev)
         def _():
             copy_b(slot).wait_recv()
 
-        keys = kv[slot, 0]
-        values = kv[slot, 1]
-        keys_t = keys.T
         q_list, do_list = [], []
         for pair in range(GROUP // 2):
             at = pair * 2 * D
-            q_pair = jnp.concatenate(
-                [q_s[slot, :, at : at + D], q_s[slot, :, at + D : at + 2 * D]], axis=0
-            )
-            do_pair = jnp.concatenate(
-                [do_s[slot, :, at : at + D], do_s[slot, :, at + D : at + 2 * D]], axis=0
-            )
-            q_list.append(q_pair)
-            do_list.append(do_pair)
-            contract = (((1,), (1,)), ((), ()))
-            scores = lax.dot_general(keys, q_pair, contract, preferred_element_type=F32)
-            scores = scores * (factor * LOG2E) + bias[...]
-            peak = jnp.max(scores, axis=0, keepdims=True)
-            weights = jnp.exp2(scores - peak)
-            total = jnp.sum(weights, axis=0, keepdims=True)
-            probs = weights * (1.0 / total)
-            rounded = probs.astype(BF16)
-            dprob = lax.dot_general(values, do_pair, contract, preferred_element_type=F32)
-            row_dot = jnp.sum(rounded.astype(F32) * dprob, axis=0, keepdims=True)
-            dscore = (probs * (dprob - row_dot)).astype(BF16)
-            span = slice(pair * 2 * rows, (pair + 1) * 2 * rows)
-            p_s[:, span] = rounded
-            ds_s[:, span] = dscore
-            grad_t = jnp.dot(keys_t, dscore, preferred_element_type=F32) * factor
-            dq_s[slot, :, at : at + D] = grad_t[:, :rows].T.astype(BF16)
-            dq_s[slot, :, at + D : at + 2 * D] = grad_t[:, rows:].T.astype(BF16)
-        store_dq(slot).start()
-
-        @pl.when(slot == mine + 1)
-        def _():
-            finish(0)
-
-        dv = jnp.dot(p_s[...], jnp.concatenate(do_list, axis=0), preferred_element_type=F32)
-        dk = jnp.dot(ds_s[...], jnp.concatenate(q_list, axis=0), preferred_element_type=F32) * factor
-        gsend[slot, 0] = dk[:length].astype(BF16)
-        gsend[slot, 1] = dv[:length].astype(BF16)
-
-        @pl.when(has_prev)
-        def _():
-            copy_d(slot).start()
-
+            q_list.append(
+                jnp.concatenate(
+                    [q_s[slot, :, at : at + D], q_s[slot, :, at + D : at + 2 * D]], axis=0
+                )
+            )
+            do_list.append(
+                jnp.concatenate(
+                    [do_s[slot, :, at : at + D], do_s[slot, :, at + D : at + 2 * D]], axis=0
+                )
+            )
+
+        def first_products(pair):
+            s_buf[pair % 2] = lax.dot_general(
+                kv[slot, 0], q_list[pair], contract, preferred_element_type=F32
+            )
+            dp_buf[pair % 2] = lax.dot_general(
+                kv[slot, 1], do_list[pair], contract, preferred_element_type=F32
+            )
+
+        def query_product(pair, keys_t):
+            span = slice(pair * wide, (pair + 1) * wide)
+            grad_t = jnp.dot(keys_t, ds_s[:, span], preferred_element_type=F32) * factor
+            grad = grad_t.astype(BF16).T
+            base = pl.multiple_of(lax.rem(mine * h + slot, heads) * width, width)
+            for n in range(2):
+                dq_ref[0, 0, :, pl.ds(base + (2 * pair + n) * D, D)] = grad[
+                    n * rows : (n + 1) * rows
+                ]
+
+        def term_products(one, two):
+            span = slice(one * wide, two * wide)
+            dk = jnp.dot(
+                ds_s[:, span],
+                jnp.concatenate(q_list[one:two], axis=0),
+                preferred_element_type=F32,
+            )
+            dv = jnp.dot(
+                p_s[:, span],
+                jnp.concatenate(do_list[one:two], axis=0),
+                preferred_element_type=F32,
+            )
+            return dk * factor, dv
+
+        keys_t = kv[slot, 0].T
+        first_products(0)
+        first_products(1)
+        softmax(0)
+        query_product(0, keys_t)
+        first_products(2)
+        softmax(1)
+        query_product(1, keys_t)
+        first_products(3)
+        dk, dv = term_products(0, 2)
         own[slot, 0] = dk[length:]
         own[slot, 1] = dv[length:]
+        part[0] = dk[:length]
+        part[1] = dv[:length]
+        softmax(2)
+        query_product(2, keys_t)
+
+        @pl.when(step == 0)
+        def _():
+            pass_on(0)
+
+        @pl.when(step == heads - 1)
+        def _():
+            finish(1)
+
+        softmax(3)
+        query_product(3, keys_t)
+        dk, dv = term_products(2, 4)
+        gsend[slot, 0] = (part[0] + dk[:length]).astype(BF16)
+        gsend[slot, 1] = (part[1] + dv[:length]).astype(BF16)
+
+        @pl.when(has_prev)
+        def _():
+            copy_d(slot).start()
+
+        own[slot, 0] += dk[length:]
+        own[slot, 1] += dv[length:]
+
+        @pl.when(step == heads - 2)
+        def _():
+            finish(0)
+
         return carry
 
-    lax.fori_loop(0, heads, one_slot, 0)
-    for j in range(1, mine):
-        finish(j)
+    lax.fori_loop(0, heads, one_step, 0)
 
     for j in range(mine):
 
@@ -267,7 +370,6 @@
         copy_a(j).wait_send()
         copy_f(j).wait_send()
     for slot in range(heads):
-        store_dq(slot).wait()
 
         @pl.when(has_next)
         def _():
@@ -276,6 +378,23 @@
         @pl.when(has_prev)
         def _():
             copy_d(slot).wait_send()
+
+
+def hand_over(dq_ref, dk_ref, dv_ref, dq_hbm, dk_hbm, dv_hbm, sem):
+    rows = dq_ref.shape[2]
+    copies = [
+        pltpu.make_async_copy(dk_ref, dk_hbm, sem.at[0]),
+        pltpu.make_async_copy(dv_ref, dv_hbm, sem.at[1]),
+    ]
+    for n in range(4):
+        at = pl.ds(n * (rows // 4), rows // 4)
+        copies.append(
+            pltpu.make_async_copy(dq_ref.at[:, :, at], dq_hbm.at[:, :, at], sem.at[2 + n])
+        )
+    for copy in copies:
+        copy.start()
+    for copy in copies:
+        copy.wait()
 
 
 def on_device(ring, query, dout, key_mant, value_mantissas, key_exps, value_exponents, reach):
@@ -283,25 +402,31 @@
     mine = key_mant.shape[3] // D
     heads = 2 * mine
     width = GROUP * D
-    hbm = pl.BlockSpec(memory_space=pl.ANY)
+    hbm = pl.BlockSpec(memory_space=pltpu.HBM)
     vmem = pl.BlockSpec(memory_space=pltpu.VMEM)
-    smem = pl.BlockSpec(memory_space=pltpu.SMEM)
     dma = pltpu.SemaphoreType.DMA
-    return pl.pallas_call(
+    out_shape = (
+        jax.ShapeDtypeStruct(query.shape, BF16),
+        jax.ShapeDtypeStruct(key_mant.shape, BF16),
+        jax.ShapeDtypeStruct(key_mant.shape, BF16),
+    )
+    grads = pl.pallas_call(
         functools.partial(kernel, ring),
-        out_shape=(
-            jax.ShapeDtypeStruct(query.shape, BF16),
-            jax.ShapeDtypeStruct(key_mant.shape, BF16),
-            jax.ShapeDtypeStruct(key_mant.shape, BF16),
-        ),
-        in_specs=[hbm, hbm, vmem, vmem, smem, smem, smem],
-        out_specs=(hbm, vmem, vmem),
+        out_shape=out_shape,
+        in_specs=[hbm] * 7,
+        out_specs=(vmem, vmem, vmem),
         scratch_shapes=[
             pltpu.VMEM((heads, rows, width), BF16),
             pltpu.VMEM((heads, rows, width), BF16),
-            pltpu.VMEM((heads, rows, width), BF16),
+            pltpu.VMEM(key_mant.shape, BF16),
+            pltpu.VMEM(key_mant.shape, BF16),
+            pltpu.SMEM(key_exps.shape, jnp.int32),
+            pltpu.SMEM(key_exps.shape, jnp.int32),
+            pltpu.SMEM(reach.shape, jnp.int32),
             pltpu.VMEM((heads, 2, 2 * length, D), BF16),
             pltpu.VMEM((2 * length, 2 * rows), F32),
+            pltpu.VMEM((2, 2 * length, 2 * rows), F32),
+            pltpu.VMEM((2, 2 * length, 2 * rows), F32),
             pltpu.VMEM((2 * length, GROUP * rows), BF16),
             pltpu.VMEM((2 * length, GROUP * rows), BF16),
             pltpu.VMEM((heads, 2, length, D), F32),
@@ -309,7 +434,8 @@
             pltpu.VMEM((heads, 2, length, D), BF16),
             pltpu.VMEM((mine, 2, length, D), BF16),
             pltpu.VMEM((mine, 2, length, D), BF16),
-            dma((heads,)),
+            pltpu.VMEM((2, length, D), F32),
+            dma((5,)),
             dma((heads,)),
             dma((heads,)),
             dma((mine,)),
@@ -330,6 +456,13 @@
             transcendentals=heads * GROUP * rows * 2 * length,
         ),
     )(query, dout, key_mant, value_mantissas, key_exps, value_exponents, reach)
+    return pl.pallas_call(
+        hand_over,
+        out_shape=out_shape,
+        in_specs=[vmem] * 3,
+        out_specs=(hbm, hbm, hbm),
+        scratch_shapes=[dma((6,))],
+    )(*grads)
 
 
 def solution(mesh):

time: 35.6 us -> 34.8 us (0.978)
  Pallas kernels: 26.8 us -> 26 us
    pallas_call x1 -> x2, Pallas kernels: 26.8 us -> 26 us  [the longest x1 23.6 us: on_device(): pl.pallas_call(functools.partial(kernel, ring), out_shape=out_shape, in_s...]
    unnamed x15 -> x18, local copies, waits for them, and re-layouts: 7.22 us -> 7.21 us
where the time goes in v2:
time: 34.8 us; the launch traced here: 34.5 us
  Pallas kernels  26 us (75%)
  local copies, waits for them, and re-layouts  7.21 us (21%)
  between operations  1.33 us (4%)
    pallas_call x1, Pallas kernels, on_device(): pl.pallas_call(functools.partial(kernel, ring), out_shape=out_shape, in_s...  23.6 us
    unnamed x18, local copies, waits for them, and re-layouts  7.21 us
    pallas_call x1, Pallas kernels, on_device(): pl.pallas_call(hand_over, out_shape=out_shape, in_specs=[vmem] * 3, out_s...  2.4 us

profile of v2, /device:TPU:1, one launch (start us, length us, event | category | flops | bytes accessed | tf_op | source)
XLA Modules:
  0.0 34.5 jit_solution(2716119361348514179)
XLA Ops:
  0.6 0.0 copy-start.7
  1.3 0.0 copy-done.7
  1.3 0.0 copy-start.3
  1.3 1.2 %copy-done.3 = bf16[1,1,128,4096]{3,2,1,0:T(8,128)(2,1)S(1)} copy-done((bf16[1,1,128,4096]{3,2,1,0:T(8,128)(2,1)S(1)}, bf16[1,1,128,4096]{3,2,1,0:T(8,128)(2,1)}, u32[]{:S(2)}) %copy-start.3) | copy-done | bytes 1048600
  2.5 0.0 copy-start.4
  2.5 1.2 %copy-done.4 = bf16[1,1,128,4096]{3,2,1,0:T(8,128)(2,1)S(1)} copy-done((bf16[1,1,128,4096]{3,2,1,0:T(8,128)(2,1)S(1)}, bf16[1,1,128,4096]{3,2,1,0:T(8,128)(2,1)}, u32[]{:S(2)}) %copy-start.4) | copy-done | bytes 1048600
  3.8 0.0 copy-start.5
  3.8 0.9 %copy-done.5 = bf16[1,1,256,256]{3,2,1,0:T(8,128)(2,1)S(1)} copy-done((bf16[1,1,256,256]{3,2,1,0:T(8,128)(2,1)S(1)}, bf16[1,1,256,256]{3,2,1,0:T(8,128)(2,1)}, u32[]{:S(2)}) %copy-start.5) | copy-done | bytes 131096
  4.7 0.0 copy-start.6
  4.7 0.9 %copy-done.6 = bf16[1,1,256,256]{3,2,1,0:T(8,128)(2,1)S(1)} copy-done((bf16[1,1,256,256]{3,2,1,0:T(8,128)(2,1)S(1)}, bf16[1,1,256,256]{3,2,1,0:T(8,128)(2,1)}, u32[]{:S(2)}) %copy-start.6) | copy-done | bytes 131096
  5.6 0.0 copy-start.8
  5.6 0.7 %copy-done.8 = s32[1,1,2,2]{3,2,1,0:T(2,128)S(1)} copy-done((s32[1,1,2,2]{3,2,1,0:T(2,128)S(1)}, s32[1,1,2,2]{3,2,1,0:T(2,128)}, u32[]{:S(2)}) %copy-start.8) | copy-done | bytes 40
  6.3 23.6 %shard_map.94 = (bf16[1,1,128,4096]{3,2,1,0:T(8,128)(2,1)S(1)}, bf16[1,1,256,256]{3,2,1,0:T(8,128)(2,1)S(1)}, bf16[1,1,256,256]{3,2,1,0:T(8,128)(2,1)S(1)}) custom-call(bf16[1,1,128,4096]{3,2,1,0:T(8,128)(2,1)S(1)} %copy-done.3, bf16[1,1,128,4096]{3,2,1,0:T(8,128)(2,1)S(1)} %copy-done.4, bf16[1,1,256,256]{3,2,1,0:T(8,128)(2,1)S(1)} %copy-done.5, ...), custom_call_target="tpu_custom_call" | custom-call | flops 2684354560 | bytes 3145728 | tf_op jit(solution)/shard_map/pallas_call | solution.py:413
  29.8 0.0 copy-start
  29.9 1.0 %copy-done = bf16[1,1,128,4096]{3,2,1,0:T(8,128)(2,1)} copy-done((bf16[1,1,128,4096]{3,2,1,0:T(8,128)(2,1)}, bf16[1,1,128,4096]{3,2,1,0:T(8,128)(2,1)S(1)}, u32[]{:S(2)}) %copy-start) | copy-done | bytes 1048600
  30.8 0.0 copy-start.1
  30.8 0.7 %copy-done.1 = bf16[1,1,256,256]{3,2,1,0:T(8,128)(2,1)} copy-done((bf16[1,1,256,256]{3,2,1,0:T(8,128)(2,1)}, bf16[1,1,256,256]{3,2,1,0:T(8,128)(2,1)S(1)}, u32[]{:S(2)}) %copy-start.1) | copy-done | bytes 131096
  31.5 0.0 copy-start.2
  31.5 0.6 %copy-done.2 = bf16[1,1,256,256]{3,2,1,0:T(8,128)(2,1)} copy-done((bf16[1,1,256,256]{3,2,1,0:T(8,128)(2,1)}, bf16[1,1,256,256]{3,2,1,0:T(8,128)(2,1)S(1)}, u32[]{:S(2)}) %copy-start.2) | copy-done | bytes 131096
  32.1 2.4 %shard_map.95 = (bf16[1,1,128,4096]{3,2,1,0:T(8,128)(2,1)}, bf16[1,1,256,256]{3,2,1,0:T(8,128)(2,1)}, bf16[1,1,256,256]{3,2,1,0:T(8,128)(2,1)}) custom-call(bf16[1,1,128,4096]{3,2,1,0:T(8,128)(2,1)} %copy-done, bf16[1,1,256,256]{3,2,1,0:T(8,128)(2,1)} %copy-done.1, bf16[1,1,256,256]{3,2,1,0:T(8,128)(2,1)} %copy-done.2), custom_call_target="tpu_custom_call" | custom-call | tf_op jit(solution)/shard_map/pallas_call | solution.py:459
Async XLA Ops:
  0.6 0.7 %copy-start.7 = (s32[1,1,2,2]{3,2,1,0:T(2,128)S(1)}, s32[1,1,2,2]{3,2,1,0:T(2,128)}, u32[]{:S(2)}) copy-start(s32[1,1,2,2]{3,2,1,0:T(2,128)} %ke_hbm.1) | copy-start | bytes 52
  1.3 1.2 %copy-start.3 = (bf16[1,1,128,4096]{3,2,1,0:T(8,128)(2,1)S(1)}, bf16[1,1,128,4096]{3,2,1,0:T(8,128)(2,1)}, u32[]{:S(2)}) copy-start(bf16[1,1,128,4096]{3,2,1,0:T(8,128)(2,1)} %q_hbm.1) | copy-start | bytes 3145732
  2.5 1.2 %copy-start.4 = (bf16[1,1,128,4096]{3,2,1,0:T(8,128)(2,1)S(1)}, bf16[1,1,128,4096]{3,2,1,0:T(8,128)(2,1)}, u32[]{:S(2)}) copy-start(bf16[1,1,128,4096]{3,2,1,0:T(8,128)(2,1)} %do_hbm.1) | copy-start | bytes 3145732
  3.8 0.9 %copy-start.5 = (bf16[1,1,256,256]{3,2,1,0:T(8,128)(2,1)S(1)}, bf16[1,1,256,256]{3,2,1,0:T(8,128)(2,1)}, u32[]{:S(2)}) copy-start(bf16[1,1,256,256]{3,2,1,0:T(8,128)(2,1)} %km_hbm.1) | copy-start | bytes 393220
  4.7 0.9 %copy-start.6 = (bf16[1,1,256,256]{3,2,1,0:T(8,128)(2,1)S(1)}, bf16[1,1,256,256]{3,2,1,0:T(8,128)(2,1)}, u32[]{:S(2)}) copy-start(bf16[1,1,256,256]{3,2,1,0:T(8,128)(2,1)} %vm_hbm.1) | copy-start | bytes 393220
  5.6 0.7 %copy-start.8 = (s32[1,1,2,2]{3,2,1,0:T(2,128)S(1)}, s32[1,1,2,2]{3,2,1,0:T(2,128)}, u32[]{:S(2)}) copy-start(s32[1,1,2,2]{3,2,1,0:T(2,128)} %ve_hbm.1) | copy-start | bytes 52
  29.8 1.0 %copy-start = (bf16[1,1,128,4096]{3,2,1,0:T(8,128)(2,1)}, bf16[1,1,128,4096]{3,2,1,0:T(8,128)(2,1)S(1)}, u32[]{:S(2)}) copy-start(bf16[1,1,128,4096]{3,2,1,0:T(8,128)(2,1)S(1)} %get-tuple-element.6.dq_ref) | copy-start | bytes 3145732
  30.8 0.7 %copy-start.1 = (bf16[1,1,256,256]{3,2,1,0:T(8,128)(2,1)}, bf16[1,1,256,256]{3,2,1,0:T(8,128)(2,1)S(1)}, u32[]{:S(2)}) copy-start(bf16[1,1,256,256]{3,2,1,0:T(8,128)(2,1)S(1)} %get-tuple-element.7.dk_ref) | copy-start | bytes 393220
  31.5 0.7 %copy-start.2 = (bf16[1,1,256,256]{3,2,1,0:T(8,128)(2,1)}, bf16[1,1,256,256]{3,2,1,0:T(8,128)(2,1)S(1)}, u32[]{:S(2)}) copy-start(bf16[1,1,256,256]{3,2,1,0:T(8,128)(2,1)S(1)} %get-tuple-element.8.dv_ref) | copy-start | bytes 393220

commit v3 on v2

--- a/solution.py
+++ b/solution.py
@@ -29,11 +29,12 @@
     ke_hbm,
     ve_hbm,
     reach_hbm,
-    dq_ref,
+    dq_hbm,
     dk_ref,
     dv_ref,
     q_s,
     do_s,
+    dq_s,
     km_ref,
     vm_ref,
     ke_ref,
@@ -42,7 +43,6 @@
     kv,
     bias,
     s_buf,
-    dp_buf,
     p_s,
     ds_s,
     own,
@@ -54,6 +54,7 @@
     in_sem,
     q_sem,
     do_sem,
+    dq_sem,
     a_send,
     a_recv,
     b_send,
@@ -87,6 +88,11 @@
             do_hbm.at[0, 0, :, columns(slot)], do_s.at[slot], do_sem.at[slot]
         )
 
+    def store_dq(slot):
+        return pltpu.make_async_copy(
+            dq_s.at[slot], dq_hbm.at[0, 0, :, columns(slot)], dq_sem.at[slot]
+        )
+
     def copy_a(j):
         return pltpu.make_async_remote_copy(
             src_ref=kv.at[j, :, pl.ds(length, length)],
@@ -214,41 +220,9 @@
 
     def fold(x, op):
         folded = x[0:8]
-        for at in range(8, chunk, 8):
+        for at in range(8, x.shape[0], 8):
             folded = op(folded, x[at : at + 8])
         return folded
-
-    def softmax(pair):
-        here = pair % 2
-        span = slice(pair * wide, (pair + 1) * wide)
-        peak = None
-        for c in range(chunks):
-            at = slice(c * chunk, (c + 1) * chunk)
-            x = s_buf[here, at] * (factor * LOG2E) + bias[at]
-            s_buf[here, at] = x
-            top = fold(x, jnp.maximum)
-            peak = top if peak is None else jnp.maximum(peak, top)
-        peak = jnp.max(peak, axis=0, keepdims=True)
-        total = None
-        for c in range(chunks):
-            at = slice(c * chunk, (c + 1) * chunk)
-            x = jnp.exp2(s_buf[here, at] - peak)
-            s_buf[here, at] = x
-            some = fold(x, jnp.add)
-            total = some if total is None else total + some
-        inverse = 1.0 / jnp.sum(total, axis=0, keepdims=True)
-        row_dot = None
-        for c in range(chunks):
-            at = slice(c * chunk, (c + 1) * chunk)
-            rounded = (s_buf[here, at] * inverse).astype(BF16)
-            p_s[at, span] = rounded
-            some = fold(rounded.astype(F32) * dp_buf[here, at], jnp.add)
-            row_dot = some if row_dot is None else row_dot + some
-        row_dot = jnp.sum(row_dot, axis=0, keepdims=True)
-        for c in range(chunks):
-            at = slice(c * chunk, (c + 1) * chunk)
-            x = (s_buf[here, at] * inverse) * (dp_buf[here, at] - row_dot)
-            ds_s[at, span] = x.astype(BF16)
 
     def one_step(step, carry):
         slot = step + (step + heads - 2) // (heads - 1) - (heads - 1) * (step // (heads - 1))
@@ -263,6 +237,8 @@
         def _():
             copy_b(slot).wait_recv()
 
+        keys_t = kv[slot, 0].T
+        values_t = kv[slot, 1].T
         q_list, do_list = [], []
         for pair in range(GROUP // 2):
             at = pair * 2 * D
@@ -277,23 +253,44 @@
                 )
             )
 
-        def first_products(pair):
-            s_buf[pair % 2] = lax.dot_general(
-                kv[slot, 0], q_list[pair], contract, preferred_element_type=F32
-            )
-            dp_buf[pair % 2] = lax.dot_general(
-                kv[slot, 1], do_list[pair], contract, preferred_element_type=F32
-            )
-
-        def query_product(pair, keys_t):
+        def scores(pair):
+            x = lax.dot_general(kv[slot, 0], q_list[pair], contract, preferred_element_type=F32)
+            x = x * (factor * LOG2E) + bias[...]
+            s_buf[pair % 2] = x
+            return jnp.max(fold(x, jnp.maximum), axis=0, keepdims=True)
+
+        def softmax(pair, peak):
+            here = pair % 2
+            span = slice(pair * wide, (pair + 1) * wide)
+            total = None
+            for c in range(chunks):
+                at = slice(c * chunk, (c + 1) * chunk)
+                x = jnp.exp2(s_buf[here, at] - peak)
+                s_buf[here, at] = x
+                some = fold(x, jnp.add)
+                total = some if total is None else total + some
+            inverse = 1.0 / jnp.sum(total, axis=0, keepdims=True)
+            for c in range(chunks):
+                at = slice(c * chunk, (c + 1) * chunk)
+                p_s[at, span] = (s_buf[here, at] * inverse).astype(BF16)
+            return inverse
+
+        def score_grads(pair, inverse):
+            here = pair % 2
+            span = slice(pair * wide, (pair + 1) * wide)
+            do_t = do_list[pair].T
+            output_t = jnp.dot(values_t, p_s[:, span], preferred_element_type=F32)
+            row_dot = jnp.sum(fold(do_t.astype(F32) * output_t, jnp.add), axis=0, keepdims=True)
+            dprob = jnp.dot(kv[slot, 1], do_t, preferred_element_type=F32)
+            ds_s[:, span] = ((s_buf[here] * inverse) * (dprob - row_dot)).astype(BF16)
+
+        def query_product(pair):
             span = slice(pair * wide, (pair + 1) * wide)
             grad_t = jnp.dot(keys_t, ds_s[:, span], preferred_element_type=F32) * factor
             grad = grad_t.astype(BF16).T
-            base = pl.multiple_of(lax.rem(mine * h + slot, heads) * width, width)
             for n in range(2):
-                dq_ref[0, 0, :, pl.ds(base + (2 * pair + n) * D, D)] = grad[
-                    n * rows : (n + 1) * rows
-                ]
+                at = (2 * pair + n) * D
+                dq_s[slot, :, at : at + D] = grad[n * rows : (n + 1) * rows]
 
         def term_products(one, two):
             span = slice(one * wide, two * wide)
@@ -309,22 +306,23 @@
             )
             return dk * factor, dv
 
-        keys_t = kv[slot, 0].T
-        first_products(0)
-        first_products(1)
-        softmax(0)
-        query_product(0, keys_t)
-        first_products(2)
-        softmax(1)
-        query_product(1, keys_t)
-        first_products(3)
+        peak = scores(0)
+        inverse = softmax(0, peak)
+        peak = scores(1)
+        score_grads(0, inverse)
+        inverse = softmax(1, peak)
+        query_product(0)
+        peak = scores(2)
+        score_grads(1, inverse)
+        inverse = softmax(2, peak)
+        query_product(1)
         dk, dv = term_products(0, 2)
         own[slot, 0] = dk[length:]
         own[slot, 1] = dv[length:]
         part[0] = dk[:length]
         part[1] = dv[:length]
-        softmax(2)
-        query_product(2, keys_t)
+        peak = scores(3)
+        score_grads(2, inverse)
 
         @pl.when(step == 0)
         def _():
@@ -334,8 +332,11 @@
         def _():
             finish(1)
 
-        softmax(3)
-        query_product(3, keys_t)
+        inverse = softmax(3, peak)
+        query_product(2)
+        score_grads(3, inverse)
+        query_product(3)
+        store_dq(slot).start()
         dk, dv = term_products(2, 4)
         gsend[slot, 0] = (part[0] + dk[:length]).astype(BF16)
         gsend[slot, 1] = (part[1] + dv[:length]).astype(BF16)
@@ -370,6 +371,7 @@
         copy_a(j).wait_send()
         copy_f(j).wait_send()
     for slot in range(heads):
+        store_dq(slot).wait()
 
         @pl.when(has_next)
         def _():
@@ -378,23 +380,6 @@
         @pl.when(has_prev)
         def _():
             copy_d(slot).wait_send()
-
-
-def hand_over(dq_ref, dk_ref, dv_ref, dq_hbm, dk_hbm, dv_hbm, sem):
-    rows = dq_ref.shape[2]
-    copies = [
-        pltpu.make_async_copy(dk_ref, dk_hbm, sem.at[0]),
-        pltpu.make_async_copy(dv_ref, dv_hbm, sem.at[1]),
-    ]
-    for n in range(4):
-        at = pl.ds(n * (rows // 4), rows // 4)
-        copies.append(
-            pltpu.make_async_copy(dq_ref.at[:, :, at], dq_hbm.at[:, :, at], sem.at[2 + n])
-        )
-    for copy in copies:
-        copy.start()
-    for copy in copies:
-        copy.wait()
 
 
 def on_device(ring, query, dout, key_mant, value_mantissas, key_exps, value_exponents, reach):
@@ -410,12 +395,13 @@
         jax.ShapeDtypeStruct(key_mant.shape, BF16),
         jax.ShapeDtypeStruct(key_mant.shape, BF16),
     )
-    grads = pl.pallas_call(
+    return pl.pallas_call(
         functools.partial(kernel, ring),
         out_shape=out_shape,
         in_specs=[hbm] * 7,
-        out_specs=(vmem, vmem, vmem),
+        out_specs=(hbm, vmem, vmem),
         scratch_shapes=[
+            pltpu.VMEM((heads, rows, width), BF16),
             pltpu.VMEM((heads, rows, width), BF16),
             pltpu.VMEM((heads, rows, width), BF16),
             pltpu.VMEM(key_mant.shape, BF16),
@@ -426,7 +412,6 @@
             pltpu.VMEM((heads, 2, 2 * length, D), BF16),
             pltpu.VMEM((2 * length, 2 * rows), F32),
             pltpu.VMEM((2, 2 * length, 2 * rows), F32),
-            pltpu.VMEM((2, 2 * length, 2 * rows), F32),
             pltpu.VMEM((2 * length, GROUP * rows), BF16),
             pltpu.VMEM((2 * length, GROUP * rows), BF16),
             pltpu.VMEM((heads, 2, length, D), F32),
@@ -438,6 +423,7 @@
             dma((5,)),
             dma((heads,)),
             dma((heads,)),
+            dma((heads,)),
             dma((mine,)),
             dma((mine,)),
             dma((heads,)),
@@ -448,7 +434,7 @@
             dma((mine,)),
         ],
         compiler_params=pltpu.CompilerParams(
-            collective_id=0, has_side_effects=True, vmem_limit_bytes=48 * 2**20
+            collective_id=0, has_side_effects=True, vmem_limit_bytes=60 * 2**20
         ),
         cost_estimate=pl.CostEstimate(
             flops=10 * heads * width * rows * 2 * length,
@@ -456,14 +442,6 @@
             transcendentals=heads * GROUP * rows * 2 * length,
         ),
     )(query, dout, key_mant, value_mantissas, key_exps, value_exponents, reach)
-    return pl.pallas_call(
-        hand_over,
-        out_shape=out_shape,
-        in_specs=[vmem] * 3,
-        out_specs=(hbm, hbm, hbm),
-        scratch_shapes=[dma((6,))],
-    )(*grads)
-
 
 def solution(mesh):
     assert mesh.shape["head"] == 2

time: 34.8 us -> 30.1 us (0.86)
  local copies, waits for them, and re-layouts: 7.21 us -> 3.93 us
  Pallas kernels: 26 us -> 24.7 us
    unnamed x18 -> x7, local copies, waits for them, and re-layouts: 7.21 us -> 3.93 us
    pallas_call x1 -> x0, Pallas kernels: 2.4 us -> none  [on_device(): pl.pallas_call(hand_over, out_shape=out_shape, in_specs=[vmem] * 3, out_s...]
    pallas_call x1, Pallas kernels: 23.6 us -> 24.7 us  [on_device(): pl.pallas_call(functools.partial(kernel, ring), out_shape=out_shape, in_s...]
where the time goes in v3:
time: 30.1 us; the launch traced here: 29.9 us
  Pallas kernels  24.7 us (82%)
  local copies, waits for them, and re-layouts  3.93 us (13%)
  between operations  1.3 us (4%)
    pallas_call x1, Pallas kernels, on_device(): pl.pallas_call(functools.partial(kernel, ring), out_shape=out_shape, in_s...  24.7 us
    unnamed x7, local copies, waits for them, and re-layouts  3.93 us

profile of v3, /device:TPU:1, one launch (start us, length us, event | category | flops | bytes accessed | tf_op | source)
XLA Modules:
  0.0 29.9 jit_solution(823311288672495968)
XLA Ops:
  1.3 24.7 %shard_map.94 = (bf16[1,1,128,4096]{3,2,1,0:T(8,128)(2,1)}, bf16[1,1,256,256]{3,2,1,0:T(8,128)(2,1)}, bf16[1,1,256,256]{3,2,1,0:T(8,128)(2,1)}) custom-call(bf16[1,1,128,4096]{3,2,1,0:T(8,128)(2,1)} %q_hbm.1, bf16[1,1,128,4096]{3,2,1,0:T(8,128)(2,1)} %do_hbm.1, bf16[1,1,256,256]{3,2,1,0:T(8,128)(2,1)} %km_hbm.1, bf16[1,1,256,256]{3,2,1,0:T(8,128)(2,1)} %vm_hbm.1, ...), custom_call_target="tpu_custom_call" | custom-call | flops 2684354560 | bytes 3145728 | tf_op jit(solution)/shard_map/pallas_call | solution.py:398
  26.0 0.0 copy-start.1
  26.0 2.3 %copy.14 = bf16[1,1,128,4096]{3,2,1,0:T(8,128)(2,1)} copy(bf16[1,1,128,4096]{3,2,1,0:T(8,128)(2,1)} %get-tuple-element.6) | data formatting | bytes 2097152
  28.3 0.0 copy-done.1
  28.3 0.0 copy-start
  28.3 0.7 %copy.15 = bf16[1,1,256,256]{3,2,1,0:T(8,128)(2,1)} copy(bf16[1,1,256,256]{3,2,1,0:T(8,128)(2,1)S(1)} %copy-done.1) | data formatting | bytes 262144
  29.0 0.3 copy-done
  29.3 0.7 %copy.16 = bf16[1,1,256,256]{3,2,1,0:T(8,128)(2,1)} copy(bf16[1,1,256,256]{3,2,1,0:T(8,128)(2,1)S(1)} %copy-done) | data formatting | bytes 262144
Async XLA Ops:
  26.0 2.3 %copy-start.1 = (bf16[1,1,256,256]{3,2,1,0:T(8,128)(2,1)S(1)}, bf16[1,1,256,256]{3,2,1,0:T(8,128)(2,1)}, u32[]{:S(2)}) copy-start(bf16[1,1,256,256]{3,2,1,0:T(8,128)(2,1)} %get-tuple-element.7) | copy-start | bytes 393220
  28.3 1.0 %copy-start = (bf16[1,1,256,256]{3,2,1,0:T(8,128)(2,1)S(1)}, bf16[1,1,256,256]{3,2,1,0:T(8,128)(2,1)}, u32[]{:S(2)}) copy-start(bf16[1,1,256,256]{3,2,1,0:T(8,128)(2,1)} %get-tuple-element.8) | copy-start | bytes 393220

commit v4 on v3

--- a/solution.py
+++ b/solution.py
@@ -29,12 +29,11 @@
     ke_hbm,
     ve_hbm,
     reach_hbm,
-    dq_hbm,
+    dq_ref,
     dk_ref,
     dv_ref,
     q_s,
     do_s,
-    dq_s,
     km_ref,
     vm_ref,
     ke_ref,
@@ -50,11 +49,9 @@
     grecv,
     fsend,
     frecv,
-    part,
     in_sem,
     q_sem,
     do_sem,
-    dq_sem,
     a_send,
     a_recv,
     b_send,
@@ -88,11 +85,6 @@
             do_hbm.at[0, 0, :, columns(slot)], do_s.at[slot], do_sem.at[slot]
         )
 
-    def store_dq(slot):
-        return pltpu.make_async_copy(
-            dq_s.at[slot], dq_hbm.at[0, 0, :, columns(slot)], dq_sem.at[slot]
-        )
-
     def copy_a(j):
         return pltpu.make_async_remote_copy(
             src_ref=kv.at[j, :, pl.ds(length, length)],
@@ -216,6 +208,7 @@
     chunk = 64
     chunks = 2 * length // chunk
     wide = 2 * rows
+    pairs = GROUP // 2
     contract = (((1,), (1,)), ((), ()))
 
     def fold(x, op):
@@ -239,114 +232,71 @@
 
         keys_t = kv[slot, 0].T
         values_t = kv[slot, 1].T
-        q_list, do_list = [], []
-        for pair in range(GROUP // 2):
-            at = pair * 2 * D
-            q_list.append(
-                jnp.concatenate(
-                    [q_s[slot, :, at : at + D], q_s[slot, :, at + D : at + 2 * D]], axis=0
-                )
+        def stacked(ref):
+            return jnp.concatenate(
+                [ref[slot, :, n * D : (n + 1) * D] for n in range(GROUP)], axis=0
             )
-            do_list.append(
-                jnp.concatenate(
-                    [do_s[slot, :, at : at + D], do_s[slot, :, at + D : at + 2 * D]], axis=0
-                )
-            )
-
-        def scores(pair):
-            x = lax.dot_general(kv[slot, 0], q_list[pair], contract, preferred_element_type=F32)
-            x = x * (factor * LOG2E) + bias[...]
-            s_buf[pair % 2] = x
-            return jnp.max(fold(x, jnp.maximum), axis=0, keepdims=True)
-
-        def softmax(pair, peak):
-            here = pair % 2
+
+        q_all = stacked(q_s)
+        do_all = stacked(do_s)
+        do_t = do_all.T
+        x = lax.dot_general(kv[slot, 0], q_all, contract, preferred_element_type=F32)
+        inverses = []
+        for pair in range(pairs):
             span = slice(pair * wide, (pair + 1) * wide)
+            some = x[:, span] * (factor * LOG2E) + bias[...]
+            s_buf[:, span] = some
+            peak = jnp.max(fold(some, jnp.maximum), axis=0, keepdims=True)
             total = None
             for c in range(chunks):
                 at = slice(c * chunk, (c + 1) * chunk)
-                x = jnp.exp2(s_buf[here, at] - peak)
-                s_buf[here, at] = x
-                some = fold(x, jnp.add)
+                weights = jnp.exp2(s_buf[at, span] - peak)
+                s_buf[at, span] = weights
+                some = fold(weights, jnp.add)
                 total = some if total is None else total + some
             inverse = 1.0 / jnp.sum(total, axis=0, keepdims=True)
+            inverses.append(inverse)
             for c in range(chunks):
                 at = slice(c * chunk, (c + 1) * chunk)
-                p_s[at, span] = (s_buf[here, at] * inverse).astype(BF16)
-            return inverse
-
-        def score_grads(pair, inverse):
-            here = pair % 2
+                p_s[at, span] = (s_buf[at, span] * inverse).astype(BF16)
+
+        @pl.when(step == 0)
+        def _():
+            pass_on(0)
+
+        output_t = jnp.dot(values_t, p_s[...], preferred_element_type=F32)
+        dprob = jnp.dot(kv[slot, 1], do_t, preferred_element_type=F32)
+        dv = jnp.dot(p_s[...], do_all, preferred_element_type=F32)
+        for pair in range(pairs):
             span = slice(pair * wide, (pair + 1) * wide)
-            do_t = do_list[pair].T
-            output_t = jnp.dot(values_t, p_s[:, span], preferred_element_type=F32)
-            row_dot = jnp.sum(fold(do_t.astype(F32) * output_t, jnp.add), axis=0, keepdims=True)
-            dprob = jnp.dot(kv[slot, 1], do_t, preferred_element_type=F32)
-            ds_s[:, span] = ((s_buf[here] * inverse) * (dprob - row_dot)).astype(BF16)
-
-        def query_product(pair):
-            span = slice(pair * wide, (pair + 1) * wide)
-            grad_t = jnp.dot(keys_t, ds_s[:, span], preferred_element_type=F32) * factor
-            grad = grad_t.astype(BF16).T
-            for n in range(2):
-                at = (2 * pair + n) * D
-                dq_s[slot, :, at : at + D] = grad[n * rows : (n + 1) * rows]
-
-        def term_products(one, two):
-            span = slice(one * wide, two * wide)
-            dk = jnp.dot(
-                ds_s[:, span],
-                jnp.concatenate(q_list[one:two], axis=0),
-                preferred_element_type=F32,
+            row_dot = jnp.sum(
+                fold(do_t[:, span].astype(F32) * output_t[:, span], jnp.add),
+                axis=0,
+                keepdims=True,
             )
-            dv = jnp.dot(
-                p_s[:, span],
-                jnp.concatenate(do_list[one:two], axis=0),
-                preferred_element_type=F32,
-            )
-            return dk * factor, dv
-
-        peak = scores(0)
-        inverse = softmax(0, peak)
-        peak = scores(1)
-        score_grads(0, inverse)
-        inverse = softmax(1, peak)
-        query_product(0)
-        peak = scores(2)
-        score_grads(1, inverse)
-        inverse = softmax(2, peak)
-        query_product(1)
-        dk, dv = term_products(0, 2)
+            ds_s[:, span] = (
+                (s_buf[:, span] * inverses[pair]) * (dprob[:, span] - row_dot)
+            ).astype(BF16)
+        own[slot, 1] = dv[length:]
+        gsend[slot, 1] = dv[:length].astype(BF16)
+
+        @pl.when(step == heads - 1)
+        def _():
+            finish(1)
+
+        dk = jnp.dot(ds_s[...], q_all, preferred_element_type=F32) * factor
+        gsend[slot, 0] = dk[:length].astype(BF16)
+
+        @pl.when(has_prev)
+        def _():
+            copy_d(slot).start()
+
         own[slot, 0] = dk[length:]
-        own[slot, 1] = dv[length:]
-        part[0] = dk[:length]
-        part[1] = dv[:length]
-        peak = scores(3)
-        score_grads(2, inverse)
-
-        @pl.when(step == 0)
-        def _():
-            pass_on(0)
-
-        @pl.when(step == heads - 1)
-        def _():
-            finish(1)
-
-        inverse = softmax(3, peak)
-        query_product(2)
-        score_grads(3, inverse)
-        query_product(3)
-        store_dq(slot).start()
-        dk, dv = term_products(2, 4)
-        gsend[slot, 0] = (part[0] + dk[:length]).astype(BF16)
-        gsend[slot, 1] = (part[1] + dv[:length]).astype(BF16)
-
-        @pl.when(has_prev)
-        def _():
-            copy_d(slot).start()
-
-        own[slot, 0] += dk[length:]
-        own[slot, 1] += dv[length:]
+        grad_t = jnp.dot(keys_t, ds_s[...], preferred_element_type=F32) * factor
+        grad = grad_t.astype(BF16).T
+        base = pl.multiple_of(lax.rem(mine * h + slot, heads) * width, width)
+        for n in range(GROUP):
+            dq_ref[0, 0, :, pl.ds(base + n * D, D)] = grad[n * rows : (n + 1) * rows]
 
         @pl.when(step == heads - 2)
         def _():
@@ -371,8 +321,6 @@
         copy_a(j).wait_send()
         copy_f(j).wait_send()
     for slot in range(heads):
-        store_dq(slot).wait()
-
         @pl.when(has_next)
         def _():
             copy_b(slot).wait_send()
@@ -391,17 +339,16 @@
     vmem = pl.BlockSpec(memory_space=pltpu.VMEM)
     dma = pltpu.SemaphoreType.DMA
     out_shape = (
-        jax.ShapeDtypeStruct(query.shape, BF16),
-        jax.ShapeDtypeStruct(key_mant.shape, BF16),
-        jax.ShapeDtypeStruct(key_mant.shape, BF16),
+        pltpu.VMEM(query.shape, BF16),
+        pltpu.VMEM(key_mant.shape, BF16),
+        pltpu.VMEM(key_mant.shape, BF16),
     )
     return pl.pallas_call(
         functools.partial(kernel, ring),
         out_shape=out_shape,
         in_specs=[hbm] * 7,
-        out_specs=(hbm, vmem, vmem),
+        out_specs=(vmem, vmem, vmem),
         scratch_shapes=[
-            pltpu.VMEM((heads, rows, width), BF16),
             pltpu.VMEM((heads, rows, width), BF16),
             pltpu.VMEM((heads, rows, width), BF16),
             pltpu.VMEM(key_mant.shape, BF16),
@@ -411,7 +358,7 @@
             pltpu.SMEM(reach.shape, jnp.int32),
             pltpu.VMEM((heads, 2, 2 * length, D), BF16),
             pltpu.VMEM((2 * length, 2 * rows), F32),
-            pltpu.VMEM((2, 2 * length, 2 * rows), F32),
+            pltpu.VMEM((2 * length, GROUP * rows), F32),
             pltpu.VMEM((2 * length, GROUP * rows), BF16),
             pltpu.VMEM((2 * length, GROUP * rows), BF16),
             pltpu.VMEM((heads, 2, length, D), F32),
@@ -419,9 +366,7 @@
             pltpu.VMEM((heads, 2, length, D), BF16),
             pltpu.VMEM((mine, 2, length, D), BF16),
             pltpu.VMEM((mine, 2, length, D), BF16),
-            pltpu.VMEM((2, length, D), F32),
             dma((5,)),
-            dma((heads,)),
             dma((heads,)),
             dma((heads,)),
             dma((mine,)),
@@ -434,7 +379,7 @@
             dma((mine,)),
         ],
         compiler_params=pltpu.CompilerParams(
-            collective_id=0, has_side_effects=True, vmem_limit_bytes=60 * 2**20
+            collective_id=0, has_side_effects=True, vmem_limit_bytes=56 * 2**20
         ),
         cost_estimate=pl.CostEstimate(
             flops=10 * heads * width * rows * 2 * length,

time: 30.1 us -> 28.6 us (0.950)
  local copies, waits for them, and re-layouts: 3.93 us -> 2.28 us
    unnamed x7 -> x3, local copies, waits for them, and re-layouts: 3.93 us -> 2.28 us
where the time goes in v4:
time: 28.6 us; the launch traced here: 28.4 us
  Pallas kernels  24.8 us (87%)
  local copies, waits for them, and re-layouts  2.28 us (8%)
  between operations  1.29 us (5%)
    pallas_call x1, Pallas kernels, on_device(): pl.pallas_call(functools.partial(kernel, ring), out_shape=out_shape, in_s...  24.8 us
    unnamed x3, local copies, waits for them, and re-layouts  2.28 us

profile of v4, /device:TPU:1, one launch (start us, length us, event | category | flops | bytes accessed | tf_op | source)
XLA Modules:
  0.0 28.4 jit_solution(18293928682942457976)
XLA Ops:
  1.3 24.8 %shard_map.94 = (bf16[1,1,128,4096]{3,2,1,0:T(8,128)(2,1)S(1)}, bf16[1,1,256,256]{3,2,1,0:T(8,128)(2,1)S(1)}, bf16[1,1,256,256]{3,2,1,0:T(8,128)(2,1)S(1)}) custom-call(bf16[1,1,128,4096]{3,2,1,0:T(8,128)(2,1)} %q_hbm.1, bf16[1,1,128,4096]{3,2,1,0:T(8,128)(2,1)} %do_hbm.1, bf16[1,1,256,256]{3,2,1,0:T(8,128)(2,1)} %km_hbm.1, bf16[1,1,256,256]{3,2,1,0:T(8,128)(2,1)} %vm_hbm.1, ...), custom_call_target="tpu_custom_call" | custom-call | flops 2684354560 | bytes 3145728 | tf_op jit(solution)/shard_map/pallas_call | solution.py:346
  26.1 1.0 %copy.13 = bf16[1,1,128,4096]{3,2,1,0:T(8,128)(2,1)} copy(bf16[1,1,128,4096]{3,2,1,0:T(8,128)(2,1)S(1)} %get-tuple-element.3) | data formatting | bytes 2097152
  27.1 0.7 %copy.14 = bf16[1,1,256,256]{3,2,1,0:T(8,128)(2,1)} copy(bf16[1,1,256,256]{3,2,1,0:T(8,128)(2,1)S(1)} %get-tuple-element.4) | data formatting | bytes 262144
  27.8 0.7 %copy.15 = bf16[1,1,256,256]{3,2,1,0:T(8,128)(2,1)} copy(bf16[1,1,256,256]{3,2,1,0:T(8,128)(2,1)S(1)} %get-tuple-element.5) | data formatting | bytes 262144

commit v5 on v4

--- a/solution.py
+++ b/solution.py
@@ -41,7 +41,10 @@
     reach_ref,
     kv,
     bias,
+    q_st,
+    do_st,
     s_buf,
+    dp_buf,
     p_s,
     ds_s,
     own,
@@ -173,7 +176,7 @@
         def _():
             copy_b(j).start()
 
-        copy_a(j).start()
+    copy_a(0).start()
 
     key_at = lax.broadcasted_iota(jnp.int32, (length, 2 * rows), 0)
     query_at = lax.rem(lax.broadcasted_iota(jnp.int32, (length, 2 * rows), 1), rows) + h * rows
@@ -222,6 +225,11 @@
         load_q(slot).wait()
         load_do(slot).wait()
 
+        @pl.when(step == 0)
+        def _():
+            copy_a(0).wait_send()
+            copy_a(1).start()
+
         @pl.when(step == 1)
         def _():
             pass_on(1)
@@ -230,61 +238,78 @@
         def _():
             copy_b(slot).wait_recv()
 
-        keys_t = kv[slot, 0].T
-        values_t = kv[slot, 1].T
-        def stacked(ref):
-            return jnp.concatenate(
-                [ref[slot, :, n * D : (n + 1) * D] for n in range(GROUP)], axis=0
+        for n in range(GROUP):
+            q_st[n] = q_s[slot, :, n * D : (n + 1) * D]
+            do_st[n] = do_s[slot, :, n * D : (n + 1) * D]
+
+        def products(pair, here):
+            q_pair = q_st[pl.ds(2 * pair, 2)].reshape(wide, D)
+            do_pair = do_st[pl.ds(2 * pair, 2)].reshape(wide, D)
+            s_buf[here] = lax.dot_general(
+                kv[slot, 0], q_pair, contract, preferred_element_type=F32
             )
-
-        q_all = stacked(q_s)
-        do_all = stacked(do_s)
-        do_t = do_all.T
-        x = lax.dot_general(kv[slot, 0], q_all, contract, preferred_element_type=F32)
-        inverses = []
-        for pair in range(pairs):
-            span = slice(pair * wide, (pair + 1) * wide)
-            some = x[:, span] * (factor * LOG2E) + bias[...]
-            s_buf[:, span] = some
-            peak = jnp.max(fold(some, jnp.maximum), axis=0, keepdims=True)
+            dp_buf[here] = lax.dot_general(
+                kv[slot, 1], do_pair, contract, preferred_element_type=F32
+            )
+
+        def softmax(pair, here):
+            peak = None
+            for c in range(chunks):
+                at = slice(c * chunk, (c + 1) * chunk)
+                x = s_buf[here, at] * (factor * LOG2E) + bias[at]
+                s_buf[here, at] = x
+                some = fold(x, jnp.maximum)
+                peak = some if peak is None else jnp.maximum(peak, some)
+            peak = jnp.max(peak, axis=0, keepdims=True)
             total = None
             for c in range(chunks):
                 at = slice(c * chunk, (c + 1) * chunk)
-                weights = jnp.exp2(s_buf[at, span] - peak)
-                s_buf[at, span] = weights
-                some = fold(weights, jnp.add)
+                x = jnp.exp2(s_buf[here, at] - peak)
+                s_buf[here, at] = x
+                some = fold(x, jnp.add)
                 total = some if total is None else total + some
             inverse = 1.0 / jnp.sum(total, axis=0, keepdims=True)
-            inverses.append(inverse)
+            row_dot = None
             for c in range(chunks):
                 at = slice(c * chunk, (c + 1) * chunk)
-                p_s[at, span] = (s_buf[at, span] * inverse).astype(BF16)
-
-        @pl.when(step == 0)
-        def _():
-            pass_on(0)
-
-        output_t = jnp.dot(values_t, p_s[...], preferred_element_type=F32)
-        dprob = jnp.dot(kv[slot, 1], do_t, preferred_element_type=F32)
-        dv = jnp.dot(p_s[...], do_all, preferred_element_type=F32)
-        for pair in range(pairs):
-            span = slice(pair * wide, (pair + 1) * wide)
-            row_dot = jnp.sum(
-                fold(do_t[:, span].astype(F32) * output_t[:, span], jnp.add),
-                axis=0,
-                keepdims=True,
-            )
-            ds_s[:, span] = (
-                (s_buf[:, span] * inverses[pair]) * (dprob[:, span] - row_dot)
-            ).astype(BF16)
+                rounded = (s_buf[here, at] * inverse).astype(BF16)
+                p_s[pair, at] = rounded
+                some = fold(rounded.astype(F32) * dp_buf[here, at], jnp.add)
+                row_dot = some if row_dot is None else row_dot + some
+            row_dot = jnp.sum(row_dot, axis=0, keepdims=True)
+            for c in range(chunks):
+                at = slice(c * chunk, (c + 1) * chunk)
+                x = (s_buf[here, at] * inverse) * (dp_buf[here, at] - row_dot)
+                ds_s[pair, at] = x.astype(BF16)
+
+        products(0, 0)
+
+        def two_pairs(n, carry):
+            products(2 * n + 1, 1)
+            softmax(2 * n, 0)
+            products(jnp.minimum(2 * n + 2, pairs - 1), 0)
+            softmax(2 * n + 1, 1)
+
+            @pl.when(jnp.logical_and(step == 0, n == 0))
+            def _():
+                pass_on(0)
+
+            return carry
+
+        lax.fori_loop(0, pairs // 2, two_pairs, 0)
+
+        @pl.when(step == heads - 1)
+        def _():
+            finish(1)
+
+        q_all = q_st[...].reshape(GROUP * rows, D)
+        do_all = do_st[...].reshape(GROUP * rows, D)
+        p_all = jnp.concatenate([p_s[n] for n in range(pairs)], axis=1)
+        ds_all = jnp.concatenate([ds_s[n] for n in range(pairs)], axis=1)
+        dv = jnp.dot(p_all, do_all, preferred_element_type=F32)
+        gsend[slot, 1] = dv[:length].astype(BF16)
         own[slot, 1] = dv[length:]
-        gsend[slot, 1] = dv[:length].astype(BF16)
-
-        @pl.when(step == heads - 1)
-        def _():
-            finish(1)
-
-        dk = jnp.dot(ds_s[...], q_all, preferred_element_type=F32) * factor
+        dk = jnp.dot(ds_all, q_all, preferred_element_type=F32) * factor
         gsend[slot, 0] = dk[:length].astype(BF16)
 
         @pl.when(has_prev)
@@ -292,9 +317,10 @@
             copy_d(slot).start()
 
         own[slot, 0] = dk[length:]
-        grad_t = jnp.dot(keys_t, ds_s[...], preferred_element_type=F32) * factor
+        keys_t = kv[slot, 0].T
+        base = pl.multiple_of(lax.rem(mine * h + slot, heads) * width, width)
+        grad_t = jnp.dot(keys_t, ds_all, preferred_element_type=F32) * factor
         grad = grad_t.astype(BF16).T
-        base = pl.multiple_of(lax.rem(mine * h + slot, heads) * width, width)
         for n in range(GROUP):
             dq_ref[0, 0, :, pl.ds(base + n * D, D)] = grad[n * rows : (n + 1) * rows]
 
@@ -317,8 +343,8 @@
         dk_ref[0, 0, :, j * D : (j + 1) * D] = total[0].astype(BF16)
         dv_ref[0, 0, :, j * D : (j + 1) * D] = total[1].astype(BF16)
 
+    copy_a(1).wait_send()
     for j in range(mine):
-        copy_a(j).wait_send()
         copy_f(j).wait_send()
     for slot in range(heads):
         @pl.when(has_next)
@@ -358,9 +384,12 @@
             pltpu.SMEM(reach.shape, jnp.int32),
             pltpu.VMEM((heads, 2, 2 * length, D), BF16),
             pltpu.VMEM((2 * length, 2 * rows), F32),
-            pltpu.VMEM((2 * length, GROUP * rows), F32),
-            pltpu.VMEM((2 * length, GROUP * rows), BF16),
-            pltpu.VMEM((2 * length, GROUP * rows), BF16),
+            pltpu.VMEM((GROUP, rows, D), BF16),
+            pltpu.VMEM((GROUP, rows, D), BF16),
+            pltpu.VMEM((2, 2 * length, 2 * rows), F32),
+            pltpu.VMEM((2, 2 * length, 2 * rows), F32),
+            pltpu.VMEM((GROUP // 2, 2 * length, 2 * rows), BF16),
+            pltpu.VMEM((GROUP // 2, 2 * length, 2 * rows), BF16),
             pltpu.VMEM((heads, 2, length, D), F32),
             pltpu.VMEM((heads, 2, length, D), BF16),
             pltpu.VMEM((heads, 2, length, D), BF16),

time: 28.6 us -> 28.9 us (1.010)
  Pallas kernels: 24.8 us -> 25.2 us
    pallas_call x1, Pallas kernels: 24.8 us -> 25.2 us  [on_device(): pl.pallas_call(functools.partial(kernel, ring), out_shape=out_shape, in_s...]
where the time goes in v5:
time: 28.9 us; the launch traced here: 28.7 us
  Pallas kernels  25.2 us (87%)
  local copies, waits for them, and re-layouts  2.28 us (8%)
  between operations  1.29 us (4%)
    pallas_call x1, Pallas kernels, on_device(): pl.pallas_call(functools.partial(kernel, ring), out_shape=out_shape, in_s...  25.2 us
    unnamed x3, local copies, waits for them, and re-layouts  2.28 us

profile of v5, /device:TPU:1, one launch (start us, length us, event | category | flops | bytes accessed | tf_op | source)
XLA Modules:
  0.0 28.7 jit_solution(5937629119076075375)
XLA Ops:
  1.3 25.2 %shard_map.94 = (bf16[1,1,128,4096]{3,2,1,0:T(8,128)(2,1)S(1)}, bf16[1,1,256,256]{3,2,1,0:T(8,128)(2,1)S(1)}, bf16[1,1,256,256]{3,2,1,0:T(8,128)(2,1)S(1)}) custom-call(bf16[1,1,128,4096]{3,2,1,0:T(8,128)(2,1)} %q_hbm.1, bf16[1,1,128,4096]{3,2,1,0:T(8,128)(2,1)} %do_hbm.1, bf16[1,1,256,256]{3,2,1,0:T(8,128)(2,1)} %km_hbm.1, bf16[1,1,256,256]{3,2,1,0:T(8,128)(2,1)} %vm_hbm.1, ...), custom_call_target="tpu_custom_call" | custom-call | flops 2684354560 | bytes 3145728 | tf_op jit(solution)/shard_map/pallas_call | solution.py:372
  26.4 1.0 %copy.13 = bf16[1,1,128,4096]{3,2,1,0:T(8,128)(2,1)} copy(bf16[1,1,128,4096]{3,2,1,0:T(8,128)(2,1)S(1)} %get-tuple-element.3) | data formatting | bytes 2097152
  27.4 0.7 %copy.14 = bf16[1,1,256,256]{3,2,1,0:T(8,128)(2,1)} copy(bf16[1,1,256,256]{3,2,1,0:T(8,128)(2,1)S(1)} %get-tuple-element.4) | data formatting | bytes 262144
  28.1 0.7 %copy.15 = bf16[1,1,256,256]{3,2,1,0:T(8,128)(2,1)} copy(bf16[1,1,256,256]{3,2,1,0:T(8,128)(2,1)S(1)} %get-tuple-element.5) | data formatting | bytes 262144

commit v6 on v5

--- a/solution.py
+++ b/solution.py
@@ -230,10 +230,6 @@
             copy_a(0).wait_send()
             copy_a(1).start()
 
-        @pl.when(step == 1)
-        def _():
-            pass_on(1)
-
         @pl.when(has_prev)
         def _():
             copy_b(slot).wait_recv()
@@ -290,13 +286,19 @@
             products(jnp.minimum(2 * n + 2, pairs - 1), 0)
             softmax(2 * n + 1, 1)
 
-            @pl.when(jnp.logical_and(step == 0, n == 0))
-            def _():
-                pass_on(0)
+            for j in range(mine):
+
+                @pl.when(jnp.logical_and(step == j, n == 0))
+                def _():
+                    pass_on(j)
 
             return carry
 
         lax.fori_loop(0, pairs // 2, two_pairs, 0)
+
+        @pl.when(step == heads - 2)
+        def _():
+            finish(0)
 
         @pl.when(step == heads - 1)
         def _():
@@ -323,10 +325,6 @@
         grad = grad_t.astype(BF16).T
         for n in range(GROUP):
             dq_ref[0, 0, :, pl.ds(base + n * D, D)] = grad[n * rows : (n + 1) * rows]
-
-        @pl.when(step == heads - 2)
-        def _():
-            finish(0)
 
         return carry
 

time: 28.9 us -> 28.6 us (0.990)
  Pallas kernels: 25.2 us -> 24.9 us
    pallas_call x1, Pallas kernels: 25.2 us -> 24.9 us  [on_device(): pl.pallas_call(functools.partial(kernel, ring), out_shape=out_shape, in_s...]
where the time goes in v6:
time: 28.6 us; the launch traced here: 28.4 us
  Pallas kernels  24.9 us (87%)
  local copies, waits for them, and re-layouts  2.28 us (8%)
  between operations  1.29 us (5%)
    pallas_call x1, Pallas kernels, on_device(): pl.pallas_call(functools.partial(kernel, ring), out_shape=out_shape, in_s...  24.9 us
    unnamed x3, local copies, waits for them, and re-layouts  2.28 us

profile of v6, /device:TPU:1, one launch (start us, length us, event | category | flops | bytes accessed | tf_op | source)
XLA Modules:
  0.0 28.4 jit_solution(1267234264136326378)
XLA Ops:
  1.3 24.9 %shard_map.94 = (bf16[1,1,128,4096]{3,2,1,0:T(8,128)(2,1)S(1)}, bf16[1,1,256,256]{3,2,1,0:T(8,128)(2,1)S(1)}, bf16[1,1,256,256]{3,2,1,0:T(8,128)(2,1)S(1)}) custom-call(bf16[1,1,128,4096]{3,2,1,0:T(8,128)(2,1)} %q_hbm.1, bf16[1,1,128,4096]{3,2,1,0:T(8,128)(2,1)} %do_hbm.1, bf16[1,1,256,256]{3,2,1,0:T(8,128)(2,1)} %km_hbm.1, bf16[1,1,256,256]{3,2,1,0:T(8,128)(2,1)} %vm_hbm.1, ...), custom_call_target="tpu_custom_call" | custom-call | flops 2684354560 | bytes 3145728 | tf_op jit(solution)/shard_map/pallas_call | solution.py:370
  26.1 1.0 %copy.13 = bf16[1,1,128,4096]{3,2,1,0:T(8,128)(2,1)} copy(bf16[1,1,128,4096]{3,2,1,0:T(8,128)(2,1)S(1)} %get-tuple-element.3) | data formatting | bytes 2097152
  27.1 0.7 %copy.14 = bf16[1,1,256,256]{3,2,1,0:T(8,128)(2,1)} copy(bf16[1,1,256,256]{3,2,1,0:T(8,128)(2,1)S(1)} %get-tuple-element.4) | data formatting | bytes 262144
  27.8 0.7 %copy.15 = bf16[1,1,256,256]{3,2,1,0:T(8,128)(2,1)} copy(bf16[1,1,256,256]{3,2,1,0:T(8,128)(2,1)S(1)} %get-tuple-element.5) | data formatting | bytes 262144

commit v7 on v6

--- a/solution.py
+++ b/solution.py
@@ -41,8 +41,8 @@
     reach_ref,
     kv,
     bias,
-    q_st,
-    do_st,
+    q_t,
+    do_t,
     s_buf,
     dp_buf,
     p_s,
@@ -193,6 +193,18 @@
     def _():
         grecv[...] = jnp.zeros_like(grecv)
 
+    def turn(slot, carry):
+        load_q(slot).wait()
+        load_do(slot).wait()
+        for n in range(GROUP):
+            at = slice(n * D, (n + 1) * D)
+            to = slice(n * rows, (n + 1) * rows)
+            q_t[slot, :, to] = q_s[slot, :, at].T
+            do_t[slot, :, to] = do_s[slot, :, at].T
+        return carry
+
+    lax.fori_loop(0, heads, turn, 0)
+
     def pass_on(j):
         copy_a(j).wait_recv()
 
@@ -212,7 +224,6 @@
     chunks = 2 * length // chunk
     wide = 2 * rows
     pairs = GROUP // 2
-    contract = (((1,), (1,)), ((), ()))
 
     def fold(x, op):
         folded = x[0:8]
@@ -222,9 +233,6 @@
 
     def one_step(step, carry):
         slot = step + (step + heads - 2) // (heads - 1) - (heads - 1) * (step // (heads - 1))
-        load_q(slot).wait()
-        load_do(slot).wait()
-
         @pl.when(step == 0)
         def _():
             copy_a(0).wait_send()
@@ -234,19 +242,15 @@
         def _():
             copy_b(slot).wait_recv()
 
-        for n in range(GROUP):
-            q_st[n] = q_s[slot, :, n * D : (n + 1) * D]
-            do_st[n] = do_s[slot, :, n * D : (n + 1) * D]
+        def stacked(ref):
+            return jnp.concatenate(
+                [ref[slot, :, n * D : (n + 1) * D] for n in range(GROUP)], axis=0
+            )
 
         def products(pair, here):
-            q_pair = q_st[pl.ds(2 * pair, 2)].reshape(wide, D)
-            do_pair = do_st[pl.ds(2 * pair, 2)].reshape(wide, D)
-            s_buf[here] = lax.dot_general(
-                kv[slot, 0], q_pair, contract, preferred_element_type=F32
-            )
-            dp_buf[here] = lax.dot_general(
-                kv[slot, 1], do_pair, contract, preferred_element_type=F32
-            )
+            span = slice(pair * wide, (pair + 1) * wide)
+            s_buf[here] = jnp.dot(kv[slot, 0], q_t[slot, :, span], preferred_element_type=F32)
+            dp_buf[here] = jnp.dot(kv[slot, 1], do_t[slot, :, span], preferred_element_type=F32)
 
         def softmax(pair, here):
             peak = None
@@ -279,22 +283,16 @@
                 ds_s[pair, at] = x.astype(BF16)
 
         products(0, 0)
-
-        def two_pairs(n, carry):
-            products(2 * n + 1, 1)
-            softmax(2 * n, 0)
-            products(jnp.minimum(2 * n + 2, pairs - 1), 0)
-            softmax(2 * n + 1, 1)
-
-            for j in range(mine):
-
-                @pl.when(jnp.logical_and(step == j, n == 0))
-                def _():
-                    pass_on(j)
-
-            return carry
-
-        lax.fori_loop(0, pairs // 2, two_pairs, 0)
+        for pair in range(pairs):
+            if pair + 1 < pairs:
+                products(pair + 1, (pair + 1) % 2)
+            softmax(pair, pair % 2)
+            if pair == 1:
+                for j in range(mine):
+
+                    @pl.when(step == j)
+                    def _():
+                        pass_on(j)
 
         @pl.when(step == heads - 2)
         def _():
@@ -304,8 +302,8 @@
         def _():
             finish(1)
 
-        q_all = q_st[...].reshape(GROUP * rows, D)
-        do_all = do_st[...].reshape(GROUP * rows, D)
+        q_all = stacked(q_s)
+        do_all = stacked(do_s)
         p_all = jnp.concatenate([p_s[n] for n in range(pairs)], axis=1)
         ds_all = jnp.concatenate([ds_s[n] for n in range(pairs)], axis=1)
         dv = jnp.dot(p_all, do_all, preferred_element_type=F32)
@@ -382,8 +380,8 @@
             pltpu.SMEM(reach.shape, jnp.int32),
             pltpu.VMEM((heads, 2, 2 * length, D), BF16),
             pltpu.VMEM((2 * length, 2 * rows), F32),
-            pltpu.VMEM((GROUP, rows, D), BF16),
-            pltpu.VMEM((GROUP, rows, D), BF16),
+            pltpu.VMEM((heads, D, GROUP * rows), BF16),
+            pltpu.VMEM((heads, D, GROUP * rows), BF16),
             pltpu.VMEM((2, 2 * length, 2 * rows), F32),
             pltpu.VMEM((2, 2 * length, 2 * rows), F32),
             pltpu.VMEM((GROUP // 2, 2 * length, 2 * rows), BF16),

time: 28.6 us -> 27.6 us (0.965)
  Pallas kernels: 24.9 us -> 23.8 us
    pallas_call x1, Pallas kernels: 24.9 us -> 23.8 us  [on_device(): pl.pallas_call(functools.partial(kernel, ring), out_shape=out_shape, in_s...]
where the time goes in v7:
time: 27.6 us; the launch traced here: 27.4 us
  Pallas kernels  23.8 us (86%)
  local copies, waits for them, and re-layouts  2.28 us (8%)
  between operations  1.29 us (5%)
    pallas_call x1, Pallas kernels, on_device(): pl.pallas_call(functools.partial(kernel, ring), out_shape=out_shape, in_s...  23.8 us
    unnamed x3, local copies, waits for them, and re-layouts  2.28 us

profile of v7, /device:TPU:1, one launch (start us, length us, event | category | flops | bytes accessed | tf_op | source)
XLA Modules:
  0.0 27.4 jit_solution(8291153400207055134)
XLA Ops:
  1.3 23.8 %shard_map.94 = (bf16[1,1,128,4096]{3,2,1,0:T(8,128)(2,1)S(1)}, bf16[1,1,256,256]{3,2,1,0:T(8,128)(2,1)S(1)}, bf16[1,1,256,256]{3,2,1,0:T(8,128)(2,1)S(1)}) custom-call(bf16[1,1,128,4096]{3,2,1,0:T(8,128)(2,1)} %q_hbm.1, bf16[1,1,128,4096]{3,2,1,0:T(8,128)(2,1)} %do_hbm.1, bf16[1,1,256,256]{3,2,1,0:T(8,128)(2,1)} %km_hbm.1, bf16[1,1,256,256]{3,2,1,0:T(8,128)(2,1)} %vm_hbm.1, ...), custom_call_target="tpu_custom_call" | custom-call | flops 2684354560 | bytes 3145728 | tf_op jit(solution)/shard_map/pallas_call | solution.py:368
  25.1 1.0 %copy.13 = bf16[1,1,128,4096]{3,2,1,0:T(8,128)(2,1)} copy(bf16[1,1,128,4096]{3,2,1,0:T(8,128)(2,1)S(1)} %get-tuple-element.3) | data formatting | bytes 2097152
  26.1 0.7 %copy.14 = bf16[1,1,256,256]{3,2,1,0:T(8,128)(2,1)} copy(bf16[1,1,256,256]{3,2,1,0:T(8,128)(2,1)S(1)} %get-tuple-element.4) | data formatting | bytes 262144
  26.7 0.7 %copy.15 = bf16[1,1,256,256]{3,2,1,0:T(8,128)(2,1)} copy(bf16[1,1,256,256]{3,2,1,0:T(8,128)(2,1)S(1)} %get-tuple-element.5) | data formatting | bytes 262144

commit v8 on v7

--- a/solution.py
+++ b/solution.py
@@ -108,22 +108,22 @@
             device_id_type=MESH,
         )
 
-    def copy_d(slot):
+    def copy_d(slot, which):
         return pltpu.make_async_remote_copy(
-            src_ref=gsend.at[slot],
-            dst_ref=grecv.at[slot],
-            send_sem=d_send.at[slot],
-            recv_sem=d_recv.at[slot],
+            src_ref=gsend.at[slot, which],
+            dst_ref=grecv.at[slot, which],
+            send_sem=d_send.at[slot, which],
+            recv_sem=d_recv.at[slot, which],
             device_id={"inner": r - 1},
             device_id_type=MESH,
         )
 
-    def copy_f(j):
+    def copy_f(j, which):
         return pltpu.make_async_remote_copy(
-            src_ref=fsend.at[j],
-            dst_ref=frecv.at[j],
-            send_sem=f_send.at[j],
-            recv_sem=f_recv.at[j],
+            src_ref=fsend.at[j, which],
+            dst_ref=frecv.at[j, which],
+            send_sem=f_send.at[j, which],
+            recv_sem=f_recv.at[j, which],
             device_id={"head": other},
             device_id_type=MESH,
         )
@@ -213,12 +213,16 @@
             copy_b(mine + j).start()
 
     def finish(j):
-        @pl.when(has_next)
-        def _():
-            copy_d(mine + j).wait_recv()
-
-        fsend[j] = (own[mine + j] + grecv[mine + j].astype(F32)).astype(BF16)
-        copy_f(j).start()
+        for which in (1, 0):
+
+            @pl.when(has_next)
+            def _():
+                copy_d(mine + j, which).wait_recv()
+
+            fsend[j, which] = (own[mine + j, which] + grecv[mine + j, which].astype(F32)).astype(
+                BF16
+            )
+            copy_f(j, which).start()
 
     chunk = 64
     chunks = 2 * length // chunk
@@ -308,13 +312,18 @@
         ds_all = jnp.concatenate([ds_s[n] for n in range(pairs)], axis=1)
         dv = jnp.dot(p_all, do_all, preferred_element_type=F32)
         gsend[slot, 1] = dv[:length].astype(BF16)
+
+        @pl.when(has_prev)
+        def _():
+            copy_d(slot, 1).start()
+
         own[slot, 1] = dv[length:]
         dk = jnp.dot(ds_all, q_all, preferred_element_type=F32) * factor
         gsend[slot, 0] = dk[:length].astype(BF16)
 
         @pl.when(has_prev)
         def _():
-            copy_d(slot).start()
+            copy_d(slot, 0).start()
 
         own[slot, 0] = dk[length:]
         keys_t = kv[slot, 0].T
@@ -328,28 +337,34 @@
 
     lax.fori_loop(0, heads, one_step, 0)
 
-    for j in range(mine):
+    for which, out_ref in ((1, dv_ref), (0, dk_ref)):
+        for j in range(mine):
+
+            @pl.when(has_next)
+            def _():
+                copy_d(j, which).wait_recv()
+
+            copy_f(j, which).wait_recv()
+            total = (
+                own[j, which] + grecv[j, which].astype(F32) + frecv[j, which].astype(F32)
+            )
+            out_ref[0, 0, :, j * D : (j + 1) * D] = total.astype(BF16)
+
+    copy_a(1).wait_send()
+    for which in range(2):
+        for j in range(mine):
+            copy_f(j, which).wait_send()
+        for slot in range(heads):
+
+            @pl.when(has_prev)
+            def _():
+                copy_d(slot, which).wait_send()
+
+    for slot in range(heads):
 
         @pl.when(has_next)
         def _():
-            copy_d(j).wait_recv()
-
-        copy_f(j).wait_recv()
-        total = own[j] + grecv[j].astype(F32) + frecv[j].astype(F32)
-        dk_ref[0, 0, :, j * D : (j + 1) * D] = total[0].astype(BF16)
-        dv_ref[0, 0, :, j * D : (j + 1) * D] = total[1].astype(BF16)
-
-    copy_a(1).wait_send()
-    for j in range(mine):
-        copy_f(j).wait_send()
-    for slot in range(heads):
-        @pl.when(has_next)
-        def _():
             copy_b(slot).wait_send()
-
-        @pl.when(has_prev)
-        def _():
-            copy_d(slot).wait_send()
 
 
 def on_device(ring, query, dout, key_mant, value_mantissas, key_exps, value_exponents, reach):
@@ -398,10 +413,10 @@
             dma((mine,)),
             dma((heads,)),
             dma((heads,)),
-            dma((heads,)),
-            dma((heads,)),
-            dma((mine,)),
-            dma((mine,)),
+            dma((heads, 2)),
+            dma((heads, 2)),
+            dma((mine, 2)),
+            dma((mine, 2)),
         ],
         compiler_params=pltpu.CompilerParams(
             collective_id=0, has_side_effects=True, vmem_limit_bytes=56 * 2**20

time: 27.6 us -> 27.4 us (level)
  no operation moved by 1% of the time
where the time goes in v8:
time: 27.4 us; the launch traced here: 27.2 us
  Pallas kernels  23.7 us (86%)
  local copies, waits for them, and re-layouts  2.28 us (8%)
  between operations  1.29 us (5%)
    pallas_call x1, Pallas kernels, on_device(): pl.pallas_call(functools.partial(kernel, ring), out_shape=out_shape, in_s...  23.7 us
    unnamed x3, local copies, waits for them, and re-layouts  2.28 us

profile of v8, /device:TPU:1, one launch (start us, length us, event | category | flops | bytes accessed | tf_op | source)
XLA Modules:
  0.0 27.2 jit_solution(5918694622286974828)
XLA Ops:
  1.3 23.7 %shard_map.94 = (bf16[1,1,128,4096]{3,2,1,0:T(8,128)(2,1)S(1)}, bf16[1,1,256,256]{3,2,1,0:T(8,128)(2,1)S(1)}, bf16[1,1,256,256]{3,2,1,0:T(8,128)(2,1)S(1)}) custom-call(bf16[1,1,128,4096]{3,2,1,0:T(8,128)(2,1)} %q_hbm.1, bf16[1,1,128,4096]{3,2,1,0:T(8,128)(2,1)} %do_hbm.1, bf16[1,1,256,256]{3,2,1,0:T(8,128)(2,1)} %km_hbm.1, bf16[1,1,256,256]{3,2,1,0:T(8,128)(2,1)} %vm_hbm.1, ...), custom_call_target="tpu_custom_call" | custom-call | flops 2684354560 | bytes 3145728 | tf_op jit(solution)/shard_map/pallas_call | solution.py:383
  25.0 1.0 %copy.13 = bf16[1,1,128,4096]{3,2,1,0:T(8,128)(2,1)} copy(bf16[1,1,128,4096]{3,2,1,0:T(8,128)(2,1)S(1)} %get-tuple-element.3) | data formatting | bytes 2097152
  25.9 0.7 %copy.14 = bf16[1,1,256,256]{3,2,1,0:T(8,128)(2,1)} copy(bf16[1,1,256,256]{3,2,1,0:T(8,128)(2,1)S(1)} %get-tuple-element.4) | data formatting | bytes 262144
  26.6 0.7 %copy.15 = bf16[1,1,256,256]{3,2,1,0:T(8,128)(2,1)} copy(bf16[1,1,256,256]{3,2,1,0:T(8,128)(2,1)S(1)} %get-tuple-element.5) | data formatting | bytes 262144
